TPU v7x, 128 devices: a whole 4x4x4 slice. The times are simulated.
128 devices in a mesh: seq: 8 (over x, core), expert: 16 (over y, z).
Axes of the slice: x: 4, y: 4, z: 4, core: 2. Of those that a mesh axis runs over, the one named last changes fastest.
Arguments:
- queries: bfloat16 [16, 1024, 4096], P('expert', 'seq'), may hold values from -6 to 6
- keys: bfloat16 [16, 1024, 512], P('expert', 'seq'), may hold values from -6 to 6
- values: bfloat16 [16, 1024, 512], P('expert', 'seq'), may hold values from -6 to 6
- w_out: bfloat16 [4096, 2048], P('seq'), may hold values from -0.09375 to 0.09375
- hidden_state: bfloat16 [16, 1024, 2048], P('expert', 'seq'), may hold values from -6 to 6
- norm_gain: bfloat16 [2048], replicated, may hold values from 0.099609375 to 1.8984375
- layer_grad: bfloat16 [16, 1024, 2048], P('expert', 'seq'), may hold values from -4 to 4
- hidden_grad: bfloat16 [16, 1024, 8, 768], P('expert', 'seq'), may hold values from -1.5 to 1.5
- routes: int32 [16, 1024, 8], P('expert', 'seq'), may hold values from 0 to 127, all different within a row; in each aligned block of 128 rows (0 to 127, 128 to 255, ..., all dimensions but the last counted through in order) at most 9 rows name the same one
- w_gate: bfloat16 [128, 2048, 768], P(('seq', 'expert')), may hold values from -0.125 to 0.125
- w_up: bfloat16 [128, 2048, 768], P(('seq', 'expert')), may hold values from -0.125 to 0.125
Outputs:
- query_grad: bfloat16 [16, 1024, 4096], P('expert', 'seq')
- key_grad: bfloat16 [16, 1024, 512], P('expert', 'seq')
- value_grad: bfloat16 [16, 1024, 512], P('expert', 'seq')
- residual_grad: bfloat16 [16, 1024, 2048], P('expert', 'seq')
- gate_grad: bfloat16 [128, 2048, 768], P(('seq', 'expert'))
- up_grad: bfloat16 [128, 2048, 768], P(('seq', 'expert'))
Inputs may be any that keep to these rules, and one draw needn't show every extreme that they name: Among the 8 routes of each of the 128 tokens of one device, no expert is named more than 9 times, and a token names 8 different experts.
All inputs are finite; a program needn't handle non-finite values.
Results may differ from a plain program's by a relative error of at most 0.017.
Values may be sent and summed in bfloat16 or wider, within the bound.
A program may use at most 128 MiB of HBM per device.

v0:
```python
import jax
import jax.numpy as jnp
from jax import lax
from jax.sharding import PartitionSpec as P

D = 2048
QUERY_HEADS = 32
KEY_VALUE_HEADS = 4
HEAD_SIZE = 128
FFE = 768
TOP = 8


def attend_heads(query_rows, key_rows, value_rows, grad_rows, query_pos, key_pos):
    factor = query_rows.shape[-1] ** (-0.5)
    scores = (
        jnp.einsum("rid,jd->rij", query_rows, key_rows, preferred_element_type=jnp.float32) * factor
    )
    allowed = key_pos[None, :] <= query_pos[:, None]
    scores = jnp.where(allowed[None], scores, -1e30)
    highest = jnp.max(scores, axis=-1, keepdims=True)
    exp_scores = jnp.exp(scores - highest)
    probs_full = exp_scores / jnp.sum(exp_scores, axis=-1, keepdims=True)
    probs_low = probs_full.astype(jnp.bfloat16)
    value_grad = jnp.einsum("rij,rid->jd", probs_low, grad_rows, preferred_element_type=jnp.float32)
    prob_grad = jnp.einsum("rid,jd->rij", grad_rows, value_rows, preferred_element_type=jnp.float32)
    delta_sum = jnp.sum(probs_full * prob_grad, axis=-1, keepdims=True)
    score_grad = (probs_full * (prob_grad - delta_sum)).astype(jnp.bfloat16)
    query_grad = (
        jnp.einsum("rij,jd->rid", score_grad, key_rows, preferred_element_type=jnp.float32) * factor
    ).astype(jnp.bfloat16)
    key_grad = (
        jnp.einsum("rij,rid->jd", score_grad, query_rows, preferred_element_type=jnp.float32)
        * factor
    )
    return (query_grad, key_grad, value_grad)


def causal_blocks(query_rows, key_rows, value_rows, grad_rows):
    length = query_rows.shape[1]
    block_rows = min(512, length)
    block_total = length // block_rows
    positions = jnp.arange(length, dtype=jnp.int32)
    query_list = []
    key_pieces = [[] for _ in range(block_total)]
    value_pieces = [[] for _ in range(block_total)]
    for block_index in range(block_total):
        lower_row = block_index * block_rows
        upper_row = lower_row + block_rows
        query_part, key_portion, value_portion = attend_heads(
            query_rows[:, lower_row:upper_row],
            key_rows[:upper_row],
            value_rows[:upper_row],
            grad_rows[:, lower_row:upper_row],
            positions[lower_row:upper_row],
            positions[:upper_row],
        )
        query_list.append(query_part)
        for key_block in range(block_index + 1):
            start_row = key_block * block_rows
            key_pieces[key_block].append(key_portion[start_row : start_row + block_rows])
            value_pieces[key_block].append(value_portion[start_row : start_row + block_rows])
    key_total = jnp.concatenate([sum(pieces[1:], pieces[0]) for pieces in key_pieces], axis=0)
    value_total = jnp.concatenate([sum(pieces[1:], pieces[0]) for pieces in value_pieces], axis=0)
    return (jnp.concatenate(query_list, axis=1), key_total, value_total)


def expert_rows(rows_in, rows_grad, gate_weight, up_weight):
    gate_pre = jnp.dot(rows_in, gate_weight, preferred_element_type=jnp.float32)
    up_pre = jnp.dot(rows_in, up_weight, preferred_element_type=jnp.float32)
    sig_gate = jax.nn.sigmoid(gate_pre)
    gate_part = (rows_grad * up_pre * sig_gate * (1.0 + gate_pre * (1.0 - sig_gate))).astype(
        jnp.bfloat16
    )
    up_part = (rows_grad * gate_pre * sig_gate).astype(jnp.bfloat16)
    rows_back = (
        jnp.dot(gate_part, gate_weight.T, preferred_element_type=jnp.float32)
        + jnp.dot(up_part, up_weight.T, preferred_element_type=jnp.float32)
    ).astype(jnp.bfloat16)
    gate_sum = lax.dot_general(
        rows_in, gate_part, (((0,), (0,)), ((), ())), preferred_element_type=jnp.float32
    )
    up_sum = lax.dot_general(
        rows_in, up_part, (((0,), (0,)), ((), ())), preferred_element_type=jnp.float32
    )
    return (rows_back, gate_sum.astype(jnp.bfloat16), up_sum.astype(jnp.bfloat16))


def attention_grads(queries, keys, values, grad_group):
    sequence_number = lax.axis_size("seq")
    resident_tokens = queries.shape[1]
    group_heads = QUERY_HEADS // sequence_number
    repeat_number = sequence_number // KEY_VALUE_HEADS
    key_resident = keys[0].reshape(resident_tokens, KEY_VALUE_HEADS, HEAD_SIZE)
    value_resident = values[0].reshape(resident_tokens, KEY_VALUE_HEADS, HEAD_SIZE)
    query_send = queries[0].reshape(resident_tokens, sequence_number, group_heads * HEAD_SIZE)
    key_send = jnp.repeat(key_resident, repeat_number, axis=1)
    value_send = jnp.repeat(value_resident, repeat_number, axis=1)
    query_all, key_all, value_all = (
        lax.all_to_all(query_send, "seq", split_axis=1, concat_axis=0, tiled=True),
        lax.all_to_all(key_send, "seq", split_axis=1, concat_axis=0, tiled=True),
        lax.all_to_all(value_send, "seq", split_axis=1, concat_axis=0, tiled=True),
    )
    length = query_all.shape[0]
    query_heads = jnp.transpose(query_all.reshape(length, group_heads, HEAD_SIZE), (1, 0, 2))
    grad_heads = jnp.transpose(grad_group.reshape(length, group_heads, HEAD_SIZE), (1, 0, 2))
    query_part, key_portion, value_portion = causal_blocks(
        query_heads,
        key_all.reshape(length, HEAD_SIZE),
        value_all.reshape(length, HEAD_SIZE),
        grad_heads,
    )
    query_rows = jnp.transpose(query_part, (1, 0, 2)).reshape(length, 1, group_heads * HEAD_SIZE)
    query_back = lax.all_to_all(query_rows, "seq", split_axis=0, concat_axis=1, tiled=True)
    key_returned, value_returned = (
        lax.all_to_all(
            key_portion.reshape(length, 1, HEAD_SIZE).astype(jnp.bfloat16),
            "seq",
            split_axis=0,
            concat_axis=1,
            tiled=True,
        ).astype(jnp.float32),
        lax.all_to_all(
            value_portion.reshape(length, 1, HEAD_SIZE).astype(jnp.bfloat16),
            "seq",
            split_axis=0,
            concat_axis=1,
            tiled=True,
        ).astype(jnp.float32),
    )
    query_out = query_back.reshape(1, resident_tokens, QUERY_HEADS * HEAD_SIZE)
    key_result = jnp.sum(
        key_returned.reshape(resident_tokens, KEY_VALUE_HEADS, repeat_number, HEAD_SIZE), axis=2
    )
    key_result = key_result.astype(jnp.bfloat16).reshape(
        1, resident_tokens, KEY_VALUE_HEADS * HEAD_SIZE
    )
    value_result = jnp.sum(
        value_returned.reshape(resident_tokens, KEY_VALUE_HEADS, repeat_number, HEAD_SIZE), axis=2
    )
    value_result = value_result.astype(jnp.bfloat16).reshape(
        1, resident_tokens, KEY_VALUE_HEADS * HEAD_SIZE
    )
    return (query_out, key_result, value_result)


def routed_grads(expert_in, hidden_grad, routes, w_gate, w_up):
    device_count = lax.axis_size(("seq", "expert"))
    resident_tokens = expert_in.shape[0]
    expert_count = w_gate.shape[0] * device_count
    capacity = max(2, 9 * resident_tokens * TOP // (8 * expert_count))
    route_flat = routes[0].reshape(-1)
    route_count = route_flat.shape[0]
    one_hot = (route_flat[:, None] == jnp.arange(expert_count, dtype=jnp.int32)[None, :]).astype(
        jnp.bfloat16
    )
    block_rows = 128
    blocked = one_hot.reshape(route_count // block_rows, block_rows, expert_count)
    lower_ones = (jnp.arange(block_rows)[:, None] > jnp.arange(block_rows)[None, :]).astype(
        jnp.bfloat16
    )
    inside = jnp.einsum("ij,bje->bie", lower_ones, blocked, preferred_element_type=jnp.float32)
    totals = jnp.sum(blocked.astype(jnp.float32), axis=1)
    offsets = jnp.cumsum(totals, axis=0) - totals
    earlier = (inside + offsets[:, None, :]).reshape(route_count, expert_count)
    rank_in_block = jnp.sum(earlier * one_hot.astype(jnp.float32), axis=1).astype(jnp.int32)
    destination = route_flat * capacity + rank_in_block
    slot_count = expert_count * capacity
    slot_route = (
        jnp.full((slot_count,), route_count, jnp.int32)
        .at[destination]
        .set(jnp.arange(route_count, dtype=jnp.int32))
    )
    input_pad = jnp.concatenate([expert_in, jnp.zeros((1, D), jnp.bfloat16)], axis=0)
    grad_pad = jnp.concatenate(
        [hidden_grad[0].reshape(route_count, FFE), jnp.zeros((1, FFE), jnp.bfloat16)], axis=0
    )
    per_device = slot_count // device_count
    send_input = input_pad[slot_route // TOP].reshape(device_count, per_device, D)
    send_grad = grad_pad[slot_route].reshape(device_count, per_device, FFE)
    got_input, got_grad = (
        lax.all_to_all(send_input, ("seq", "expert"), split_axis=0, concat_axis=0, tiled=True),
        lax.all_to_all(send_grad, ("seq", "expert"), split_axis=0, concat_axis=0, tiled=True),
    )
    rows_in = got_input.reshape(device_count * capacity, D)
    rows_grad = got_grad.reshape(device_count * capacity, FFE)
    rows_back, gate_sum, up_sum = expert_rows(rows_in, rows_grad, w_gate[0], w_up[0])
    back_list = rows_back.reshape(device_count, capacity, D)
    gate_list = [gate_sum]
    up_list = [up_sum]
    got_back = lax.all_to_all(back_list, ("seq", "expert"), split_axis=0, concat_axis=0, tiled=True)
    got_back = got_back.reshape(slot_count, D)
    token_rows = got_back[destination].reshape(resident_tokens, TOP, D).astype(jnp.float32)
    routed_grad = jnp.sum(token_rows, axis=1)
    return (routed_grad, jnp.stack(gate_list, axis=0), jnp.stack(up_list, axis=0))


def local(
    queries,
    keys,
    values,
    w_out,
    hidden_state,
    norm_gain,
    layer_grad,
    hidden_grad,
    routes,
    w_gate,
    w_up,
):
    resident_tokens = hidden_state.shape[1]
    state_full = hidden_state[0].astype(jnp.float32)
    rstd = lax.rsqrt(jnp.mean(state_full * state_full, axis=-1, keepdims=True) + 1e-06)
    normed = state_full * rstd
    gain_full = norm_gain.astype(jnp.float32)
    expert_in = (normed * gain_full).astype(jnp.bfloat16)
    routed_grad, gate_grad, up_grad = routed_grads(expert_in, hidden_grad, routes, w_gate, w_up)
    weighted = gain_full * routed_grad
    inner = jnp.mean(weighted * normed, axis=-1, keepdims=True)
    residual_rows = (layer_grad[0].astype(jnp.float32) + rstd * (weighted - normed * inner)).astype(
        jnp.bfloat16
    )
    grad_group = lax.dot_general(
        lax.all_gather(residual_rows, "seq", axis=0, tiled=True),
        w_out,
        (((1,), (1,)), ((), ())),
        preferred_element_type=jnp.float32,
    ).astype(jnp.bfloat16)
    query_out, key_result, value_result = attention_grads(queries, keys, values, grad_group)
    residual_grad = residual_rows.reshape(1, resident_tokens, D)
    return (query_out, key_result, value_result, residual_grad, gate_grad, up_grad)


def solution(mesh):
    return jax.shard_map(
        local,
        mesh=mesh,
        in_specs=(
            P("expert", "seq", None),
            P("expert", "seq", None),
            P("expert", "seq", None),
            P("seq", None),
            P("expert", "seq", None),
            P(),
            P("expert", "seq", None),
            P("expert", "seq", None, None),
            P("expert", "seq", None),
            P(("seq", "expert"), None, None),
            P(("seq", "expert"), None, None),
        ),
        out_specs=(
            P("expert", "seq", None),
            P("expert", "seq", None),
            P("expert", "seq", None),
            P("expert", "seq", None),
            P(("seq", "expert"), None, None),
            P(("seq", "expert"), None, None),
        ),
        check_vma=False,
    )
```

profile of v0, /device:TPU:1, one launch (start us, length us, event | category | flops | bytes accessed | tf_op | source)
XLA Modules:
  0.0 549.0 jit_solution(13723071417122634779)
XLA Ops:
  9.7 4.3 scatter_custom_fusion
  14.1 2.7 concatenate.39
  16.7 7.3 %gather_fusion = bf16[1152,768]{1,0:T(8,128)(2,1)} fusion(bf16[1025,768]{1,0:T(8,128)(2,1)} %concatenate.39, s32[2048]{0:T(1024)S(1)} %get-tuple-element.37), kind=kCustom, calls=%fused_computation | custom fusion | bytes 3543552 | tf_op jit(solution)/shard_map/gather | solution.py:180
  24.1 4.2 reshape.357
  28.2 11.9 %all-to-all-start.2 = ((bf16[128,9,768]{2,1,0:T(8,128)(2,1)}), bf16[128,9,768]{2,1,0:T(8,128)(2,1)}, u32[]{:S(2)}, u32[]{:S(2)}) async-start(bf16[128,9,768]{2,1,0:T(8,128)(2,1)} %reshape.357), calls=%async_computation.2 | async-start | bytes 6291456 | tf_op jit(solution)/shard_map/all_to_all | solution.py:183
  43.5 11.8 %gather_fusion.1 = bf16[1152,2048]{1,0:T(8,128)(2,1)} fusion(bf16[129,2048]{1,0:T(8,128)(2,1)} %concatenate.40, s32[2048]{0:T(1024)S(1)} %get-tuple-element.36), kind=kCustom, calls=%fused_computation.1 | custom fusion | bytes 9441792 | tf_op jit(solution)/shard_map/gather | solution.py:179
  55.3 8.1 %reshape.358 = bf16[128,9,2048]{2,1,0:T(8,128)(2,1)} reshape(bf16[1152,2048]{1,0:T(8,128)(2,1)} %gather_fusion.1) | data formatting | bytes 9437184 | tf_op jit(solution)/shard_map/reshape | solution.py:179
  63.4 17.3 %all-to-all-done.2 = bf16[128,9,768]{2,1,0:T(8,128)(2,1)} async-done(((bf16[128,9,768]{2,1,0:T(8,128)(2,1)}), bf16[128,9,768]{2,1,0:T(8,128)(2,1)}, u32[]{:S(2)}, u32[]{:S(2)}) %all-to-all-start.2) | async-done | bytes 1769504 | tf_op jit(solution)/shard_map/all_to_all | solution.py:183
  80.7 6.7 %all-to-all-start.3 = ((bf16[128,9,2048]{2,1,0:T(8,128)(2,1)}), bf16[128,9,2048]{2,1,0:T(8,128)(2,1)}, u32[]{:S(2)}, u32[]{:S(2)}) async-start(bf16[128,9,2048]{2,1,0:T(8,128)(2,1)} %reshape.358), calls=%async_computation.3 | async-start | bytes 16777216 | tf_op jit(solution)/shard_map/all_to_all | solution.py:182
  87.4 4.6 reshape.370
  92.0 101.2 %all-to-all-done.3 = bf16[128,9,2048]{2,1,0:T(8,128)(2,1)} async-done(((bf16[128,9,2048]{2,1,0:T(8,128)(2,1)}), bf16[128,9,2048]{2,1,0:T(8,128)(2,1)}, u32[]{:S(2)}, u32[]{:S(2)}) %all-to-all-start.3) | async-done | bytes 4718624 | tf_op jit(solution)/shard_map/all_to_all | solution.py:182
  193.2 8.5 %reshape.359 = bf16[1152,2048]{1,0:T(8,128)(2,1)} reshape(bf16[128,9,2048]{2,1,0:T(8,128)(2,1)} %all-to-all-done.3) | data formatting | bytes 9437184 | tf_op jit(solution)/shard_map/reshape | solution.py:185
  201.7 7.9 %multiply_convert_fusion.2 = (bf16[1152,768]{1,0:T(8,128)(2,1)S(1)}, f32[1152,768]{1,0:T(8,128)S(1)}) fusion(f32[1152,768]{1,0:T(8,128)} %reshape.370, bf16[1152,2048]{1,0:T(8,128)(2,1)} %reshape.359, bf16[1,2048,768]{2,1,0:T(8,128)(2,1)S(1)} %copy-done), kind=kOutput, calls=%fused_computation.26 | convolution fusion | flops 3629187072 | bytes 16711680 | tf_op jit(solution)/shard_map/dot_general | solution.py:69
  209.7 4.8 fusion.10
  214.5 3.9 fusion.12
  218.4 5.6 %add_convert_fusion = bf16[1152,2048]{1,0:T(8,128)(2,1)} fusion(f32[1152,2048]{1,0:T(8,128)S(1)} %fusion.12, bf16[1152,768]{1,0:T(8,128)(2,1)S(1)} %get-tuple-element.26, bf16[1,2048,768]{2,1,0:T(8,128)(2,1)S(1)} %copy-done.26), kind=kOutput, calls=%fused_computation.6 | convolution fusion | flops 3628597248 | bytes 19070976 | tf_op jit(solution)/shard_map/dot_general | solution.py:78
  224.0 8.1 %reshape.360 = bf16[128,9,2048]{2,1,0:T(8,128)(2,1)} reshape(bf16[1152,2048]{1,0:T(8,128)(2,1)} %add_convert_fusion) | data formatting | bytes 9437184 | tf_op jit(solution)/shard_map/reshape | solution.py:188
  232.1 9.0 %all-to-all-start.4 = ((bf16[128,9,2048]{2,1,0:T(8,128)(2,1)}), bf16[128,9,2048]{2,1,0:T(8,128)(2,1)}, u32[]{:S(2)}, u32[]{:S(2)}) async-start(bf16[128,9,2048]{2,1,0:T(8,128)(2,1)} %reshape.360), calls=%async_computation.4 | async-start | bytes 16777216 | tf_op jit(solution)/shard_map/all_to_all | solution.py:191
  241.2 105.1 %all-to-all-done.4 = bf16[128,9,2048]{2,1,0:T(8,128)(2,1)} async-done(((bf16[128,9,2048]{2,1,0:T(8,128)(2,1)}), bf16[128,9,2048]{2,1,0:T(8,128)(2,1)}, u32[]{:S(2)}, u32[]{:S(2)}) %all-to-all-start.4) | async-done | bytes 4718624 | tf_op jit(solution)/shard_map/all_to_all | solution.py:191
  346.3 8.5 %reshape.361 = bf16[1152,2048]{1,0:T(8,128)(2,1)} reshape(bf16[128,9,2048]{2,1,0:T(8,128)(2,1)} %all-to-all-done.4) | data formatting | bytes 9437184 | tf_op jit(solution)/shard_map/reshape | solution.py:192
  354.8 11.8 %gather_fusion.2 = bf16[1024,2048]{1,0:T(8,128)(2,1)} fusion(bf16[1152,2048]{1,0:T(8,128)(2,1)} %reshape.361, s32[1024]{0:T(1024)S(1)} %broadcast_clamp_fusion), kind=kCustom, calls=%fused_computation.2 | custom fusion | bytes 8392704 | tf_op jit(solution)/shard_map/gather | solution.py:193
  366.6 5.1 convert_reduce_fusion
  374.1 5.1 all-to-all-start.1
  381.7 4.0 all-to-all-done.1
  386.5 5.0 all-to-all-start.5
  392.7 8.6 %all-to-all-done.5 = bf16[128,8,128]{2,0,1:T(8,128)(2,1)} async-done(((bf16[128,8,128]{2,0,1:T(8,128)(2,1)}), bf16[128,8,128]{2,0,1:T(8,128)(2,1)}, u32[]{:S(2)}, u32[]{:S(2)}) %all-to-all-start.5) | async-done | bytes 262176 | tf_op jit(solution)/shard_map/all_to_all | solution.py:102
  401.3 4.4 all-to-all-start
  409.4 12.0 %all-to-all-done = bf16[128,8,512]{0,2,1:T(8,128)(2,1)S(1)} async-done(((bf16[128,8,512]{0,2,1:T(8,128)(2,1)}), bf16[128,8,512]{0,2,1:T(8,128)(2,1)S(1)}, u32[]{:S(2)}, u32[]{:S(2)}) %all-to-all-start) | async-done | bytes 1048608 | tf_op jit(solution)/shard_map/all_to_all | solution.py:100
  427.7 4.0 fusion.104
  431.7 7.2 %fusion.99 = (f32[4,512]{1,0:T(4,128)}, f32[4,512,1024]{2,1,0:T(8,128)}) fusion(pred[512,1024]{1,0:T(8,128)(4,1)} %iota_compare_fusion, bf16[1024,128,1]{1,0,2:T(8,128)(2,1)S(1)} %bitcast.192, bf16[4,1024,128]{2,1,0:T(8,128)(2,1)S(1)} %bitcast.178), kind=kOutput, calls=%fused_computation.139 | convolution fusion | flops 545260544 | bytes 9707520 | tf_op jit(solution)/shard_map/sub | solution.py:22
  438.9 8.9 %fusion.18 = bf16[1,2048,768]{2,1,0:T(8,128)(2,1)} fusion(bf16[1152,2048]{1,0:T(8,128)(2,1)} %reshape.359, bf16[1152,768]{1,0:T(8,128)(2,1)} %copy-done.27), kind=kOutput, calls=%fused_computation.38 | convolution fusion | flops 3625451520 | bytes 9633792 | tf_op jit(solution)/shard_map/dot_general | solution.py:80
  447.8 6.2 %convolution_convert_fusion.2 = bf16[1024,512]{0,1:T(8,128)(2,1)} fusion(bf16[1024,2048]{1,0:T(8,128)(2,1)} %all-gather.2.cloned.1.call-done, bf16[512,2048]{1,0:T(8,128)(2,1)} %param.14), kind=kOutput, calls=%fused_computation.47 | convolution fusion | flops 2148007936 | bytes 7340032 | tf_op jit(solution)/shard_map/dot_general | solution.py:223
  454.0 2.3 copy.72
  456.3 5.3 fusion.32
  462.5 3.3 multiply_reduce_fusion.1
  469.5 4.4 all-to-all-start.8
  473.9 5.1 multiply_reduce_fusion
  482.7 2.6 copy-done.6
  490.1 3.5 fusion.31
  493.6 4.8 all-to-all-start.7
  498.4 2.4 fusion.30
  503.3 2.1 reduce.3
  508.5 5.0 all-to-all-start.6
  513.5 8.9 %fusion.19 = bf16[1,2048,768]{2,1,0:T(8,128)(2,1)} fusion(bf16[1152,2048]{1,0:T(8,128)(2,1)} %reshape.359, bf16[1152,768]{1,0:T(8,128)(2,1)} %copy-done.28), kind=kOutput, calls=%fused_computation.39 | convolution fusion | flops 3625451520 | bytes 9633792 | tf_op jit(solution)/shard_map/dot_general | solution.py:83
  528.7 5.9 %reshape.418 = bf16[1024,1,512]{2,1,0:T(2,128)(2,1)} reshape(bf16[8,2,32768]{2,1,0:T(2,128)(2,1)} %all-to-all-done.6) | data formatting | bytes 2097152
  534.6 2.8 copy.90
  537.4 2.3 copy.77
  539.7 2.3 copy.84
  (139 shorter events, 47.7 us)
Async XLA Ops:
  7.2 194.6 %copy-start = (bf16[1,2048,768]{2,1,0:T(8,128)(2,1)S(1)}, bf16[1,2048,768]{2,1,0:T(8,128)(2,1)}, u32[]{:S(2)}) copy-start(bf16[1,2048,768]{2,1,0:T(8,128)(2,1)} %param.20) | copy-start | bytes 9437188
  28.2 11.9 %copy-start.23 = (bf16[2048]{0:T(1024)(128)(2,1)S(1)}, bf16[2048]{0:T(1024)(128)(2,1)}, u32[]{:S(2)}) copy-start(bf16[2048]{0:T(1024)(128)(2,1)} %param.16) | copy-start | bytes 12292
  28.2 52.5 %all-to-all-start.2 = ((bf16[128,9,768]{2,1,0:T(8,128)(2,1)}), bf16[128,9,768]{2,1,0:T(8,128)(2,1)}, u32[]{:S(2)}, u32[]{:S(2)}) async-start(bf16[128,9,768]{2,1,0:T(8,128)(2,1)} %reshape.357), calls=%async_computation.2 | async-start | bytes 6291456 | tf_op jit(solution)/shard_map/all_to_all | solution.py:183
  41.4 330.6 %copy-start.21 = (f32[128]{0:T(128)}, f32[128]{0:T(128)S(1)}, u32[]{:S(2)}) copy-start(f32[128]{0:T(128)S(1)} %add_rsqrt_fusion) | copy-start | bytes 1540
  80.7 112.5 %all-to-all-start.3 = ((bf16[128,9,2048]{2,1,0:T(8,128)(2,1)}), bf16[128,9,2048]{2,1,0:T(8,128)(2,1)}, u32[]{:S(2)}, u32[]{:S(2)}) async-start(bf16[128,9,2048]{2,1,0:T(8,128)(2,1)} %reshape.358), calls=%async_computation.3 | async-start | bytes 16777216 | tf_op jit(solution)/shard_map/all_to_all | solution.py:182
  201.7 7.9 %copy-start.4 = (bf16[1152,2048]{1,0:T(8,128)(2,1)S(1)}, bf16[1152,2048]{1,0:T(8,128)(2,1)}, u32[]{:S(2)}) copy-start(bf16[1152,2048]{1,0:T(8,128)(2,1)} %reshape.359) | copy-start | bytes 14155780
  201.7 7.9 %copy-start.9 = (f32[1152,768]{1,0:T(8,128)S(1)}, f32[1152,768]{1,0:T(8,128)}, u32[]{:S(2)}) copy-start(f32[1152,768]{1,0:T(8,128)} %reshape.370) | copy-start | bytes 10616836
  201.7 7.9 %copy-start.26 = (bf16[1,2048,768]{2,1,0:T(8,128)(2,1)S(1)}, bf16[1,2048,768]{2,1,0:T(8,128)(2,1)}, u32[]{:S(2)}) copy-start(bf16[1,2048,768]{2,1,0:T(8,128)(2,1)} %param.21) | copy-start | bytes 9437188
  209.6 8.7 %copy-start.28 = (bf16[1152,768]{1,0:T(8,128)(2,1)}, bf16[1152,768]{1,0:T(8,128)(2,1)S(1)}, u32[]{:S(2)}) copy-start(bf16[1152,768]{1,0:T(8,128)(2,1)S(1)} %get-tuple-element.26) | copy-start | bytes 5308420
  214.5 3.9 copy-start.27
  232.1 114.2 %all-to-all-start.4 = ((bf16[128,9,2048]{2,1,0:T(8,128)(2,1)}), bf16[128,9,2048]{2,1,0:T(8,128)(2,1)}, u32[]{:S(2)}, u32[]{:S(2)}) async-start(bf16[128,9,2048]{2,1,0:T(8,128)(2,1)} %reshape.360), calls=%async_computation.4 | async-start | bytes 16777216 | tf_op jit(solution)/shard_map/all_to_all | solution.py:191
  241.2 206.6 %all-gather.2.cloned.1.call-start = ((), (), s32[]{:S(2)}) async-start(), calls=%async_computation.9 | async-start | bytes 4718592 | tf_op jit(solution)/shard_map/all_gather | solution.py:224
  366.6 5.1 copy-start.2
  366.6 5.5 copy-start.11
  366.6 6.7 %copy-start.16 = (bf16[1,128,512]{2,1,0:T(8,128)(2,1)S(1)}, bf16[1,128,512]{2,1,0:T(8,128)(2,1)}, u32[]{:S(2)}) copy-start(bf16[1,128,512]{2,1,0:T(8,128)(2,1)} %param.12) | copy-start | bytes 393220
  371.7 19.7 %copy-start.12 = (bf16[1,128,4096]{2,1,0:T(8,128)(2,1)S(1)}, bf16[1,128,4096]{2,1,0:T(8,128)(2,1)}, u32[]{:S(2)}) copy-start(bf16[1,128,4096]{2,1,0:T(8,128)(2,1)} %param.11) | copy-start | bytes 3145732
  372.1 1.2 copy-start.24
  374.1 11.6 %all-to-all-start.1 = ((bf16[128,8,128]{2,0,1:T(8,128)(2,1)}), bf16[128,8,128]{2,0,1:T(8,128)(2,1)S(1)}, u32[]{:S(2)}, u32[]{:S(2)}) async-start(bf16[128,8,128]{2,0,1:T(8,128)(2,1)} %bitcast.4), calls=%async_computation.1 | async-start | bytes 524288 | tf_op jit(solution)/shard_map/all_to_all | solution.py:101
  385.7 46.0 %copy-start.14 = (bf16[128,8,128]{2,0,1:T(8,128)(2,1)}, bf16[128,8,128]{2,0,1:T(8,128)(2,1)S(1)}, u32[]{:S(2)}) copy-start(bf16[128,8,128]{2,0,1:T(8,128)(2,1)S(1)} %all-to-all-done.1) | copy-start | bytes 786436
  386.5 14.8 %all-to-all-start.5 = ((bf16[128,8,128]{2,0,1:T(8,128)(2,1)}), bf16[128,8,128]{2,0,1:T(8,128)(2,1)}, u32[]{:S(2)}, u32[]{:S(2)}) async-start(bf16[128,8,128]{2,0,1:T(8,128)(2,1)} %bitcast.21), calls=%async_computation.5 | async-start | bytes 524288 | tf_op jit(solution)/shard_map/all_to_all | solution.py:102
  401.3 20.1 %all-to-all-start = ((bf16[128,8,512]{0,2,1:T(8,128)(2,1)}), bf16[128,8,512]{0,2,1:T(8,128)(2,1)S(1)}, u32[]{:S(2)}, u32[]{:S(2)}) async-start(bf16[128,8,512]{0,2,1:T(8,128)(2,1)} %bitcast), calls=%async_computation | async-start | bytes 2097152 | tf_op jit(solution)/shard_map/all_to_all | solution.py:100
  425.9 1.8 copy-start.15
  427.7 4.0 copy-start.10
  447.8 8.5 %copy-start.18 = (f32[4,512]{1,0:T(4,128)S(1)}, f32[4,512]{1,0:T(4,128)}, u32[]{:S(2)}) copy-start(f32[4,512]{1,0:T(4,128)} %get-tuple-element.28) | copy-start | bytes 24580
  456.3 5.3 copy-start.5
  456.3 5.3 copy-start.13
  461.6 0.9 copy-start.17
  469.5 24.1 %all-to-all-start.8 = ((bf16[8,2,8192]{2,1,0:T(2,128)(2,1)}), bf16[8,2,8192]{2,1,0:T(2,128)(2,1)S(1)}, u32[]{:S(2)}, u32[]{:S(2)}) async-start(bf16[8,2,8192]{2,1,0:T(2,128)(2,1)} %reshape.421), calls=%async_computation.8 | async-start | bytes 524288 | tf_op jit(solution)/shard_map/all_to_all | solution.py:123
  473.9 5.2 slice-start
  473.9 6.1 %slice-start.1 = ((s8[8388608]{0:T(1024)(128)(4,1)}), s8[4194304]{0:T(1024)(128)(4,1)S(1)}, s32[]{:S(2)}) async-start(s8[8388608]{0:T(1024)(128)(4,1)} %bitcast.171), calls=%async_computation.11 | async-start | bytes 8388608
  473.9 6.1 %copy-start.19 = (f32[4,512]{1,0:T(4,128)S(1)}, f32[4,512]{1,0:T(4,128)}, u32[]{:S(2)}) copy-start(f32[4,512]{1,0:T(4,128)} %get-tuple-element.28) | copy-start | bytes 24580
  480.0 2.7 copy-start.7
  481.4 5.1 copy-start.8
  481.4 3.9 copy-start.6
  481.4 3.9 copy-start.20
  486.5 1.3 copy-start.3
  493.6 14.9 %all-to-all-start.7 = ((bf16[8,2,8192]{2,1,0:T(2,128)(2,1)}), bf16[8,2,8192]{2,1,0:T(2,128)(2,1)}, u32[]{:S(2)}, u32[]{:S(2)}) async-start(bf16[8,2,8192]{2,1,0:T(2,128)(2,1)} %reshape.419), calls=%async_computation.7 | async-start | bytes 524288 | tf_op jit(solution)/shard_map/all_to_all | solution.py:116
  508.5 20.2 %all-to-all-start.6 = ((bf16[8,2,32768]{2,1,0:T(2,128)(2,1)}), bf16[8,2,32768]{2,1,0:T(2,128)(2,1)}, u32[]{:S(2)}, u32[]{:S(2)}) async-start(bf16[8,2,32768]{2,1,0:T(2,128)(2,1)} %reshape.417), calls=%async_computation.6 | async-start | bytes 2097152 | tf_op jit(solution)/shard_map/all_to_all | solution.py:114
  513.5 8.9 %copy-start.22 = (f32[128]{0:T(128)S(1)}, f32[128]{0:T(128)}, u32[]{:S(2)}) copy-start(f32[128]{0:T(128)} %copy-done.21) | copy-start | bytes 1540
  513.5 8.9 %copy-start.25 = (f32[128]{0:T(128)S(1)}, f32[128]{0:T(128)}, u32[]{:S(2)}) copy-start(f32[128]{0:T(128)} %copy-done.24) | copy-start | bytes 1540
  528.7 13.3 %copy-start.1 = (bf16[1,2048,768]{2,1,0:T(8,128)(2,1)S(1)}, bf16[1,2048,768]{2,1,0:T(8,128)(2,1)}, u32[]{:S(2)}) copy-start(bf16[1,2048,768]{2,1,0:T(8,128)(2,1)} %param.20) | copy-start | bytes 9437188
Sparse Core Ops, SparseCore 0:
  373.4 39.1 all-gather.1
where the time goes:
time: 559 us; the launch traced here: 549 us
  waiting for transfers between devices  250 us (45%)
  local copies, waits for them, and re-layouts  125 us (22%)
  matrix products  77.7 us (14%)
  starting transfers between devices  56.3 us (10%)
  other arithmetic  25.4 us (5%)
  between operations  14.9 us (3%)
    all_to_all x1, waiting for transfers between devices, routed_grads(): lax.all_to_all(back_list, ('seq', 'expert'), split_axis=0, concat_axis=0,...  105 us
    all_to_all x1, waiting for transfers between devices, routed_grads(): lax.all_to_all(send_input, ('seq', 'expert'), split_axis=0, concat_axis=0...  101 us
    unnamed x77, local copies, waits for them, and re-layouts  27 us
    all_to_all x1, waiting for transfers between devices, routed_grads(): lax.all_to_all(send_grad, ('seq', 'expert'), split_axis=0, concat_axis=0,...  17.3 us
    all_to_all x1, waiting for transfers between devices, attention_grads(): lax.all_to_all(query_send, 'seq', split_axis=1, concat_axis=0, tiled=True)  12 us
    all_to_all x1, starting transfers between devices, routed_grads(): lax.all_to_all(send_grad, ('seq', 'expert'), split_axis=0, concat_axis=0,...  11.9 us
    gather x1, local copies, waits for them, and re-layouts, routed_grads(): input_pad[slot_route // TOP].reshape(device_count, per_device, D)  11.8 us
    gather x1, local copies, waits for them, and re-layouts, routed_grads(): got_back[destination].reshape(resident_tokens, TOP, D).astype(jnp.float32)  11.8 us
  transfers between devices with their start and end apart: 10, of which 7 were waited for; matrix products, arithmetic and copies ran while one was open for 18% of the time, Pallas kernels for 0%

commit v1 on v0

v1 whole, which is shorter than its diff:
```python
import functools

import jax
import jax.numpy as jnp
from jax import lax
from jax.experimental import pallas as pl
from jax.experimental.pallas import tpu as pltpu
from jax.sharding import PartitionSpec as P

D = 2048
QUERY_HEADS = 32
KEY_VALUE_HEADS = 4
HEAD_SIZE = 128
FFE = 768
TOP = 8
LOG2E = 1.4426950408889634

NN = (((1,), (0,)), ((), ()))
NT = (((1,), (1,)), ((), ()))
TN = (((0,), (0,)), ((), ()))


def dot(a, b, dims):
    return lax.dot_general(a, b, dims, preferred_element_type=jnp.float32)


def attention_kernel(heads, block, qkv_ref, res_ref, w_ref, out_ref, grad, key_t, dk, dv):
    length = qkv_ref.shape[0]
    width = heads * HEAD_SIZE
    factor = HEAD_SIZE ** (-0.5)
    for lower in range(0, length, block):
        rows = pl.ds(lower, block)
        grad[rows, :] = dot(res_ref[rows, :], w_ref[...], NT).astype(jnp.bfloat16)
    key_t[...] = qkv_ref[:, width : width + HEAD_SIZE].astype(jnp.float32).T.astype(jnp.bfloat16)
    dk[...] = jnp.zeros_like(dk)
    dv[...] = jnp.zeros_like(dv)
    for lower in range(0, length, block):
        rows, upper = pl.ds(lower, block), lower + block
        key_pos = lax.broadcasted_iota(jnp.int32, (block, block), 0)
        query_pos = lax.broadcasted_iota(jnp.int32, (block, block), 1)
        for head in range(heads):
            columns = pl.ds(head * HEAD_SIZE, HEAD_SIZE)
            query, out_grad = qkv_ref[rows, columns], grad[rows, columns]
            keys = qkv_ref[0:upper, width : width + HEAD_SIZE]
            values = qkv_ref[0:upper, width + HEAD_SIZE : width + 2 * HEAD_SIZE]
            scores = dot(keys, query, NT) * (factor * LOG2E)
            last = jnp.where(key_pos <= query_pos, scores[lower:upper], -1e30)
            scores = last if lower == 0 else jnp.concatenate([scores[:lower], last], axis=0)
            exps = jnp.exp2(scores - jnp.max(scores, axis=0, keepdims=True))
            probs = exps * (1.0 / jnp.sum(exps, axis=0, keepdims=True))
            dv[0:upper, :] += dot(probs.astype(jnp.bfloat16), out_grad, NN)
            prob_grad = dot(values, out_grad, NT)
            delta = jnp.sum(probs * prob_grad, axis=0, keepdims=True)
            score_grad = (probs * (prob_grad - delta)).astype(jnp.bfloat16)
            dk[0:upper, :] += dot(score_grad, query, NN)
            query_grad = dot(key_t[:, 0:upper], score_grad, NN) * factor
            out_ref[rows, columns] = query_grad.T.astype(jnp.bfloat16)
    out_ref[:, width : width + HEAD_SIZE] = (dk[...] * factor).astype(jnp.bfloat16)
    out_ref[:, width + HEAD_SIZE : width + 2 * HEAD_SIZE] = dv[...].astype(jnp.bfloat16)


def attention_core(qkv, residual, w_out):
    length, heads = qkv.shape[0], w_out.shape[0] // HEAD_SIZE
    return pl.pallas_call(
        functools.partial(attention_kernel, heads, min(256, length)),
        out_shape=jax.ShapeDtypeStruct(qkv.shape, jnp.bfloat16),
        in_specs=[pl.BlockSpec(memory_space=pltpu.VMEM)] * 3,
        out_specs=pl.BlockSpec(memory_space=pltpu.VMEM),
        scratch_shapes=[
            pltpu.VMEM((length, heads * HEAD_SIZE), jnp.bfloat16),
            pltpu.VMEM((HEAD_SIZE, length), jnp.bfloat16),
            pltpu.VMEM((length, HEAD_SIZE), jnp.float32),
            pltpu.VMEM((length, HEAD_SIZE), jnp.float32),
        ],
        compiler_params=pltpu.CompilerParams(vmem_limit_bytes=48 << 20),
        cost_estimate=pl.CostEstimate(
            flops=9_000_000_000, bytes_accessed=10_000_000, transcendentals=3_000_000
        ),
        name="attention_core",
    )(qkv, residual, w_out)


def exchange_heads(queries, keys, values):
    group = lax.axis_size("seq")
    tokens = queries.shape[1]
    repeat = group // KEY_VALUE_HEADS
    query_send = jnp.transpose(queries[0].reshape(tokens, group, -1), (1, 0, 2))

    def spread(array):
        by_head = jnp.transpose(array[0].reshape(tokens, KEY_VALUE_HEADS, HEAD_SIZE), (1, 0, 2))
        return jnp.repeat(by_head, repeat, axis=0)

    send = jnp.concatenate([query_send, spread(keys), spread(values)], axis=-1)
    got = lax.all_to_all(send, "seq", split_axis=0, concat_axis=0, tiled=True)
    return got.reshape(group * tokens, -1)


def return_heads(grads):
    group = lax.axis_size("seq")
    tokens = grads.shape[0] // group
    width = grads.shape[1] - 2 * HEAD_SIZE
    got = lax.all_to_all(
        grads.reshape(group, tokens, -1), "seq", split_axis=0, concat_axis=0, tiled=True
    )
    query_out = jnp.transpose(got[:, :, :width], (1, 0, 2)).reshape(1, tokens, group * width)

    def total(part):
        part = part.astype(jnp.float32).reshape(KEY_VALUE_HEADS, -1, tokens, HEAD_SIZE)
        part = jnp.sum(part, axis=1).astype(jnp.bfloat16)
        return jnp.transpose(part, (1, 0, 2)).reshape(1, tokens, KEY_VALUE_HEADS * HEAD_SIZE)

    return (
        query_out,
        total(got[:, :, width : width + HEAD_SIZE]),
        total(got[:, :, width + HEAD_SIZE :]),
    )


def expert_rows(rows_in, rows_grad, gate_weight, up_weight):
    gate_pre = dot(rows_in, gate_weight, NN)
    up_pre = dot(rows_in, up_weight, NN)
    sig_gate = jax.nn.sigmoid(gate_pre)
    gate_part = (rows_grad * up_pre * sig_gate * (1.0 + gate_pre * (1.0 - sig_gate))).astype(
        jnp.bfloat16
    )
    up_part = (rows_grad * gate_pre * sig_gate).astype(jnp.bfloat16)
    rows_back = (dot(gate_part, gate_weight, NT) + dot(up_part, up_weight, NT)).astype(jnp.bfloat16)
    gate_sum = dot(rows_in, gate_part, TN)
    up_sum = dot(rows_in, up_part, TN)
    return (rows_back, gate_sum.astype(jnp.bfloat16), up_sum.astype(jnp.bfloat16))


def routed_grads(expert_in, hidden_grad, routes, w_gate, w_up):
    devices = lax.axis_size(("seq", "expert"))
    tokens = expert_in.shape[0]
    route = routes[0]
    named = route[:, :, None] == jnp.arange(devices, dtype=jnp.int32)
    count = jnp.sum(named.astype(jnp.bfloat16), axis=1)
    earlier = (jnp.arange(tokens)[:, None] > jnp.arange(tokens)[None, :]).astype(jnp.bfloat16)
    rank = dot(earlier, count, NN)
    route_rank = jnp.sum(jnp.where(named, rank[:, None, :], 0.0), axis=2).astype(jnp.int32)
    slots = jnp.arange(8, dtype=jnp.float32)
    rank_t = jnp.where(count > 0, rank, -1.0).T
    token_main = (rank_t[:, None, :] == slots[None, :, None]).astype(jnp.bfloat16)
    token_main = token_main.reshape(devices * 8, tokens)
    token_last = (rank_t == 8.0).astype(jnp.bfloat16)
    place_main = jnp.where(route_rank < 8, route * 8 + route_rank, -1).reshape(1, -1)
    place_last = jnp.where(route_rank == 8, route, -1).reshape(1, -1)
    route_main = (place_main == jnp.arange(devices * 8, dtype=jnp.int32)[:, None]).astype(
        jnp.bfloat16
    )
    route_last = (place_last == jnp.arange(devices, dtype=jnp.int32)[:, None]).astype(jnp.bfloat16)
    grads = hidden_grad[0].reshape(tokens * TOP, FFE)
    send_main = jnp.concatenate(
        [
            dot(token_main, expert_in, NN).astype(jnp.bfloat16),
            dot(route_main, grads, NN).astype(jnp.bfloat16),
        ],
        axis=1,
    )
    last_in = dot(token_last, expert_in, NN).astype(jnp.bfloat16)
    last_grad = dot(route_last, grads, NN).astype(jnp.bfloat16)
    last_grad = jnp.pad(last_grad.reshape(devices, 6, 128), ((0, 0), (0, 2), (0, 0)))
    send = jnp.concatenate(
        [
            send_main.reshape(devices, 8, D + FFE),
            last_in.reshape(devices, 8, D // 8),
            last_grad,
        ],
        axis=2,
    )
    got = lax.all_to_all(send, ("seq", "expert"), split_axis=0, concat_axis=0, tiled=True)
    rows_in = jnp.concatenate(
        [
            got[:, :, :D].reshape(devices * 8, D),
            got[:, :, D + FFE : D + FFE + D // 8].reshape(devices, D),
        ],
        axis=0,
    )
    rows_grad = jnp.concatenate(
        [
            got[:, :, D : D + FFE].reshape(devices * 8, FFE),
            got[:, :6, D + FFE + D // 8 :].reshape(devices, FFE),
        ],
        axis=0,
    )
    rows_back, gate_sum, up_sum = expert_rows(rows_in, rows_grad, w_gate[0], w_up[0])
    back_send = jnp.concatenate(
        [
            rows_back[: devices * 8].reshape(devices, 8, D),
            rows_back[devices * 8 :].reshape(devices, 8, D // 8),
        ],
        axis=2,
    )
    back = lax.all_to_all(back_send, ("seq", "expert"), split_axis=0, concat_axis=0, tiled=True)
    routed_grad = dot(token_main, back[:, :, :D].reshape(devices * 8, D), TN)
    routed_grad += dot(token_last, back[:, :, D:].reshape(devices, D), TN)
    return (routed_grad, gate_sum[None], up_sum[None])


def local(
    queries,
    keys,
    values,
    w_out,
    hidden_state,
    norm_gain,
    layer_grad,
    hidden_grad,
    routes,
    w_gate,
    w_up,
):
    state_full = hidden_state[0].astype(jnp.float32)
    rstd = lax.rsqrt(jnp.mean(state_full * state_full, axis=-1, keepdims=True) + 1e-06)
    normed = state_full * rstd
    gain_full = norm_gain.astype(jnp.float32)
    expert_in = (normed * gain_full).astype(jnp.bfloat16)
    routed_grad, gate_grad, up_grad = routed_grads(expert_in, hidden_grad, routes, w_gate, w_up)
    qkv = exchange_heads(queries, keys, values)
    weighted = gain_full * routed_grad
    inner = jnp.mean(weighted * normed, axis=-1, keepdims=True)
    residual_rows = (layer_grad[0].astype(jnp.float32) + rstd * (weighted - normed * inner)).astype(
        jnp.bfloat16
    )
    residual_all = lax.all_gather(residual_rows, "seq", axis=0, tiled=True)
    grads = attention_core(qkv, residual_all, w_out)
    query_out, key_out, value_out = return_heads(grads)
    return (query_out, key_out, value_out, residual_rows[None], gate_grad, up_grad)


def solution(mesh):
    return jax.shard_map(
        local,
        mesh=mesh,
        in_specs=(
            P("expert", "seq", None),
            P("expert", "seq", None),
            P("expert", "seq", None),
            P("seq", None),
            P("expert", "seq", None),
            P(),
            P("expert", "seq", None),
            P("expert", "seq", None, None),
            P("expert", "seq", None),
            P(("seq", "expert"), None, None),
            P(("seq", "expert"), None, None),
        ),
        out_specs=(
            P("expert", "seq", None),
            P("expert", "seq", None),
            P("expert", "seq", None),
            P("expert", "seq", None),
            P(("seq", "expert"), None, None),
            P(("seq", "expert"), None, None),
        ),
        check_vma=False,
    )
```

time: 559 us -> 335 us (0.60)
  waiting for transfers between devices: 250 us -> 36.9 us
  blocking collectives: 0 us -> 155 us
  local copies, waits for them, and re-layouts: 125 us -> 30.1 us
  starting transfers between devices: 56.3 us -> 9.78 us
  matrix products: 77.7 us -> 54.6 us
  Pallas kernels: 0 us -> 17.8 us
  other arithmetic: 25.4 us -> 10.3 us
    all_to_all x9 -> x2, waiting for transfers between devices: 250 us -> 36.9 us  [the longest x1 26 us: exchange_heads(): got = lax.all_to_all(send, 'seq', split_axis=0, concat_axis=0, tiled=True)]
    all_to_all x0 -> x2, blocking collectives: none -> 155 us  [the longest x1 90.3 us: routed_grads(): lax.all_to_all(send, ('seq', 'expert'), split_axis=0, concat_axis=0, tile...]
    all_to_all x9 -> x2, starting transfers between devices: 56.3 us -> 9.74 us  [the longest x1 4.99 us: exchange_heads(): got = lax.all_to_all(send, 'seq', split_axis=0, concat_axis=0, tiled=True)]
    reshape x9 -> x5, local copies, waits for them, and re-layouts: 43 us -> 9.21 us  [the longest x1 2.82 us: routed_grads(): got[:, :, :D].reshape(devices * 8, D)]
    gather x3 -> x0, local copies, waits for them, and re-layouts: 30.9 us -> none  [the longest x1 11.8 us: routed_grads(): input_pad[slot_route // TOP].reshape(device_count, per_device, D)]
    pallas_call x0 -> x1, Pallas kernels: none -> 17.8 us  [attention_core(): pl.pallas_call(functools.partial(attention_kernel, heads, min(256, length...]
    dot_general x17 -> x13, matrix products: 70.5 us -> 54.6 us  [dot(): return lax.dot_general(a, b, dims, preferred_element_type=jnp.float32)]
    unnamed x77 -> x47, local copies, waits for them, and re-layouts: 27 us -> 13.6 us
  transfers between devices with their start and end apart: 10 -> 3, of which waited for: 7 -> 2; matrix products, arithmetic and copies ran while one was open for 18% -> 7% of each run, Pallas kernels for 0% -> 0%
where the time goes in v1:
time: 335 us; the launch traced here: 329 us
  blocking collectives  155 us (46%)
  matrix products  54.6 us (16%)
  waiting for transfers between devices  36.9 us (11%)
  local copies, waits for them, and re-layouts  30.1 us (9%)
  Pallas kernels  17.8 us (5%)
  between operations  14.7 us (4%)
  other arithmetic  10.3 us (3%)
  starting transfers between devices  9.78 us (3%)
    all_to_all x1, blocking collectives, routed_grads(): lax.all_to_all(send, ('seq', 'expert'), split_axis=0, concat_axis=0, tile...  90.3 us
    all_to_all x1, blocking collectives, routed_grads(): lax.all_to_all(back_send, ('seq', 'expert'), split_axis=0, concat_axis=0,...  64.6 us
    dot_general x13, matrix products, dot(): return lax.dot_general(a, b, dims, preferred_element_type=jnp.float32)  54.6 us
    all_to_all x1, waiting for transfers between devices, exchange_heads(): got = lax.all_to_all(send, 'seq', split_axis=0, concat_axis=0, tiled=True)  26 us
    pallas_call x1, Pallas kernels, attention_core(): pl.pallas_call(functools.partial(attention_kernel, heads, min(256, length...  17.8 us
    unnamed x47, local copies, waits for them, and re-layouts  13.6 us
    all_to_all x1, waiting for transfers between devices, return_heads(): lax.all_to_all(grads.reshape(group, tokens, -1), 'seq', split_axis=0, con...  10.9 us
  transfers between devices with their start and end apart: 3, of which 2 were waited for; matrix products, arithmetic and copies ran while one was open for 7% of the time, Pallas kernels for 0%

profile of v1, /device:TPU:1, one launch (start us, length us, event | category | flops | bytes accessed | tf_op | source)
XLA Modules:
  0.0 329.1 jit_solution(6621791609991712115)
XLA Ops:
  7.2 0.9 copy.92
  8.9 0.8 copy.94
  9.8 1.2 fusion.41
  11.1 0.7 convert_element_type.105
  12.0 4.5 %convolution_convert_fusion = bf16[1024,2048]{1,0:T(8,128)(2,1)} fusion(bf16[1,128,2048]{2,1,0:T(8,128)(2,1)} %param.15, f32[2048]{0:T(1024)S(1)} %convert_element_type.105, f32[128]{0:T(128)S(1)} %add_rsqrt_fusion, f32[128,128]{1,0:T(8,128)S(1)} %copy.93), kind=kOutput, calls=%fused_computation.17 | convolution fusion | flops 540147712 | bytes 4792832 | tf_op jit(solution)/shard_map/dot_general | solution.py:24
  16.5 0.4 convolution_convert_fusion.3
  16.8 0.9 copy.110
  17.8 3.1 fusion.23
  21.3 0.8 copy.96
  22.1 1.1 copy.108
  23.2 3.2 maximum_bitcast_fusion
  26.4 0.6 fusion.1
  27.0 90.3 %all_to_all.20 = bf16[128,8,3200]{2,1,0:T(8,128)(2,1)S(1)} all-to-all(bf16[128,8,3200]{2,1,0:T(8,128)(2,1)S(1)} %fusion.1), channel_id=1, replica_groups=mesh['seq'=8,'expert'=16] {'seq','expert'}, dimensions={0} | all-to-all | bytes 13107200 | tf_op jit(solution)/shard_map/all_to_all | solution.py:172
  117.3 1.1 copy.111
  118.3 1.8 copy-done.3
  120.1 0.9 copy.107
  121.0 1.1 copy.99
  122.1 2.8 slice_bitcast_fusion.1
  125.0 3.8 %fusion.12 = f32[1152,768]{1,0:T(8,128)S(1)} fusion(bf16[1,2048,768]{2,1,0:T(8,128)(2,1)S(1)} %copy-done, bf16[128,2048]{1,0:T(8,128)(2,1)S(1)} %bitcast.125, bf16[1024,2048]{1,0:T(8,128)(2,1)S(1)} %slice_bitcast_fusion.1), kind=kOutput, calls=%fused_computation.26 | convolution fusion | flops 3633315840 | bytes 11403264 | tf_op jit(solution)/shard_map/dot_general | solution.py:24
  128.8 2.7 slice_bitcast_fusion.2
  131.5 6.0 %fusion.9 = bf16[1152,768]{1,0:T(8,128)(2,1)S(1)} fusion(f32[1152,768]{1,0:T(8,128)S(1)} %fusion.12, bf16[1,2048,768]{2,1,0:T(8,128)(2,1)S(1)} %copy-done.16, bf16[128,768]{1,0:T(8,128)(2,1)S(1)} %copy.99, bf16[1024,768]{1,0:T(8,128)(2,1)S(1)} %slice_bitcast_fusion.2, bf16[128,2048]{1,0:T(8,128)(2,1)S(1)} %bitcast.126, ...), kind=kOutput, calls=%fused_computation.23 | convolution fusion | flops 3645702144 | bytes 14942208 | tf_op jit(solution)/shard_map/dot_general | solution.py:24
  137.6 1.2 copy-done.18
  138.8 6.3 %fusion.10 = f32[1152,2048]{1,0:T(8,128)} fusion(bf16[1152,768]{1,0:T(8,128)(2,1)S(1)} %fusion.9, bf16[1,2048,768]{2,1,0:T(8,128)(2,1)S(1)} %copy-done), kind=kOutput, calls=%fused_computation.24 | convolution fusion | flops 3623878656 | bytes 14352384 | tf_op jit(solution)/shard_map/dot_general | solution.py:24
  145.1 7.7 %add_convert_fusion = bf16[1152,2048]{1,0:T(8,128)(2,1)S(1)} fusion(f32[1152,2048]{1,0:T(8,128)} %fusion.10, bf16[1,2048,768]{2,1,0:T(8,128)(2,1)S(1)} %copy-done.16, f32[1152,768]{1,0:T(8,128)} %copy-done.17, bf16[128,768]{1,0:T(8,128)(2,1)S(1)} %copy.99, bf16[1024,768]{1,0:T(8,128)(2,1)S(1)} %slice_bitcast_fusion.2), kind=kOutput, calls=%fused_computation.2 | convolution fusion | flops 3637444608 | bytes 22609920 | tf_op jit(solution)/shard_map/dot_general | solution.py:24
  153.4 0.4 pad_maximum_fusion.1
  153.8 64.6 %all_to_all.21 = bf16[128,8,2304]{2,1,0:T(8,128)(2,1)S(1)} all-to-all(bf16[128,8,2304]{2,1,0:T(8,128)(2,1)S(1)} %pad_maximum_fusion.1), channel_id=1, replica_groups=mesh['seq'=8,'expert'=16] {'seq','expert'}, dimensions={0} | all-to-all | bytes 9437184 | tf_op jit(solution)/shard_map/all_to_all | solution.py:195
  218.4 2.1 copy-done.6
  220.6 0.4 copy.100
  221.0 3.0 fusion.18
  224.1 0.5 fusion.36
  224.6 1.2 fusion.40
  225.8 0.4 copy.109
  226.6 0.9 reshape_squeeze.14
  227.7 1.3 pad_maximum_fusion.3
  229.0 5.0 %all-to-all-start = ((bf16[8,128,768]{2,1,0:T(8,128)(2,1)}), bf16[8,128,768]{2,1,0:T(8,128)(2,1)S(1)}, u32[]{:S(2)}, u32[]{:S(2)}) async-start(bf16[8,128,768]{2,1,0:T(8,128)(2,1)} %pad_maximum_fusion.3), calls=%async_computation | async-start | bytes 3145728 | tf_op jit(solution)/shard_map/all_to_all | solution.py:94
  234.0 8.8 %fusion.16 = bf16[1,2048,768]{2,1,0:T(8,128)(2,1)} fusion(bf16[1152,768]{1,0:T(8,128)(2,1)} %copy-done.18, bf16[128,2048]{1,0:T(8,128)(2,1)S(1)} %bitcast.127, bf16[1024,2048]{1,0:T(8,128)(2,1)} %copy-done.7), kind=kOutput, calls=%fused_computation.30 | convolution fusion | flops 3634888704 | bytes 9633792 | tf_op jit(solution)/shard_map/dot_general | solution.py:24
  242.7 26.0 %all-to-all-done = bf16[8,128,768]{2,1,0:T(8,128)(2,1)S(1)} async-done(((bf16[8,128,768]{2,1,0:T(8,128)(2,1)}), bf16[8,128,768]{2,1,0:T(8,128)(2,1)S(1)}, u32[]{:S(2)}, u32[]{:S(2)}) %all-to-all-start) | async-done | bytes 1572896 | tf_op jit(solution)/shard_map/all_to_all | solution.py:94
  268.7 1.6 copy-done.2
  270.3 17.8 %attention_core.1 = bf16[1024,768]{1,0:T(8,128)(2,1)} custom-call(bf16[1024,768]{1,0:T(8,128)(2,1)S(1)} %bitcast.109, bf16[1024,2048]{1,0:T(8,128)(2,1)} %all-gather.2.cloned.1.call-done.res_ref, bf16[512,2048]{1,0:T(8,128)(2,1)S(1)} %copy-done.2), custom_call_target="tpu_custom_call" | custom-call | flops 8999999488 | bytes 10000000 | tf_op jit(solution)/shard_map/attention_core/pallas_call | solution.py:64
  288.1 4.8 %all-to-all-start.3 = ((bf16[8,128,768]{2,1,0:T(8,128)(2,1)}), bf16[8,128,768]{2,1,0:T(8,128)(2,1)}, u32[]{:S(2)}, u32[]{:S(2)}) async-start(bf16[8,128,768]{2,1,0:T(8,128)(2,1)} %bitcast.23), calls=%async_computation.3 | async-start | bytes 3145728 | tf_op jit(solution)/shard_map/all_to_all | solution.py:102
  292.9 10.0 %fusion.17 = bf16[1,2048,768]{2,1,0:T(8,128)(2,1)} fusion(bf16[128,2048]{1,0:T(8,128)(2,1)} %bitcast.124, bf16[1024,2048]{1,0:T(8,128)(2,1)} %copy-done.7, f32[1152,768]{1,0:T(8,128)} %copy-done.17, bf16[128,768]{1,0:T(8,128)(2,1)S(1)} %copy.99, bf16[1024,768]{1,0:T(8,128)(2,1)} %copy-done.10), kind=kOutput, calls=%fused_computation.31 | convolution fusion | flops 3643736064 | bytes 13172736 | tf_op jit(solution)/shard_map/dot_general | solution.py:24
  302.9 10.9 %all-to-all-done.3 = bf16[8,128,768]{2,1,0:T(8,128)(2,1)} async-done(((bf16[8,128,768]{2,1,0:T(8,128)(2,1)}), bf16[8,128,768]{2,1,0:T(8,128)(2,1)}, u32[]{:S(2)}, u32[]{:S(2)}) %all-to-all-start.3) | async-done | bytes 1572896 | tf_op jit(solution)/shard_map/all_to_all | solution.py:102
  313.7 1.5 slice_bitcast_fusion.3
  315.2 1.6 copy.101
  316.8 2.3 reshape.181
  319.1 1.1 bitcast_reduce_fusion
  320.4 0.8 copy.104
  321.3 0.8 copy.105
  (63 shorter events, 2.9 us)
Async XLA Ops:
  7.2 117.8 %copy-start = (bf16[1,2048,768]{2,1,0:T(8,128)(2,1)S(1)}, bf16[1,2048,768]{2,1,0:T(8,128)(2,1)}, u32[]{:S(2)}) copy-start(bf16[1,2048,768]{2,1,0:T(8,128)(2,1)} %param.20) | copy-start | bytes 9437188
  7.2 261.6 %all-gather.2.cloned.1.call-start = ((), (), s32[]{:S(2)}) async-start(), calls=%async_computation.4 | async-start | bytes 4718592 | tf_op jit(solution)/shard_map/all_gather | solution.py:226
  12.0 4.5 %copy-start.4 = (bf16[1,128,2048]{2,1,0:T(8,128)(2,1)S(1)}, bf16[1,128,2048]{2,1,0:T(8,128)(2,1)}, u32[]{:S(2)}) copy-start(bf16[1,128,2048]{2,1,0:T(8,128)(2,1)} %param.15) | copy-start | bytes 1572868
  12.0 5.8 %copy-start.9 = (bf16[1,128,8,768]{3,2,1,0:T(8,128)(2,1)S(1)}, bf16[1,128,8,768]{3,2,1,0:T(8,128)(2,1)}, u32[]{:S(2)}) copy-start(bf16[1,128,8,768]{3,2,1,0:T(8,128)(2,1)} %param.18) | copy-start | bytes 4718596
  23.2 3.2 copy-start.8
  117.2 2.9 copy-start.3
  122.1 2.9 copy-start.13
  124.9 6.6 %copy-start.7 = (bf16[1024,2048]{1,0:T(8,128)(2,1)}, bf16[1024,2048]{1,0:T(8,128)(2,1)S(1)}, u32[]{:S(2)}) copy-start(bf16[1024,2048]{1,0:T(8,128)(2,1)S(1)} %slice_bitcast_fusion.1) | copy-start | bytes 12582916
  124.9 6.6 %copy-start.16 = (bf16[1,2048,768]{2,1,0:T(8,128)(2,1)S(1)}, bf16[1,2048,768]{2,1,0:T(8,128)(2,1)}, u32[]{:S(2)}) copy-start(bf16[1,2048,768]{2,1,0:T(8,128)(2,1)} %param.21) | copy-start | bytes 9437188
  128.8 8.8 %copy-start.17 = (f32[1152,768]{1,0:T(8,128)}, f32[1152,768]{1,0:T(8,128)S(1)}, u32[]{:S(2)}) copy-start(f32[1152,768]{1,0:T(8,128)S(1)} %fusion.12) | copy-start | bytes 10616836
  131.5 13.6 %copy-start.10 = (bf16[1024,768]{1,0:T(8,128)(2,1)}, bf16[1024,768]{1,0:T(8,128)(2,1)S(1)}, u32[]{:S(2)}) copy-start(bf16[1024,768]{1,0:T(8,128)(2,1)S(1)} %slice_bitcast_fusion.2) | copy-start | bytes 4718596
  137.6 1.2 copy-start.18
  218.4 2.1 copy-start.6
  220.5 3.5 %copy-start.5 = (bf16[1,128,2048]{2,1,0:T(8,128)(2,1)S(1)}, bf16[1,128,2048]{2,1,0:T(8,128)(2,1)}, u32[]{:S(2)}) copy-start(bf16[1,128,2048]{2,1,0:T(8,128)(2,1)} %param.15) | copy-start | bytes 1572868
  221.0 3.5 %copy-start.12 = (bf16[1,128,2048]{2,1,0:T(8,128)(2,1)S(1)}, bf16[1,128,2048]{2,1,0:T(8,128)(2,1)}, u32[]{:S(2)}) copy-start(bf16[1,128,2048]{2,1,0:T(8,128)(2,1)} %param.17) | copy-start | bytes 1572868
  224.0 1.7 copy-start.11
  224.5 2.0 copy-start.15
  227.6 6.4 %copy-start.14 = (bf16[16,8,8,256]{3,1,2,0:T(8,128)(2,1)S(1)}, bf16[16,8,8,256]{3,1,2,0:T(8,128)(2,1)}, u32[]{:S(2)}) copy-start(bf16[16,8,8,256]{3,1,2,0:T(8,128)(2,1)} %copy.111) | copy-start | bytes 1572868
  229.0 39.8 %all-to-all-start = ((bf16[8,128,768]{2,1,0:T(8,128)(2,1)}), bf16[8,128,768]{2,1,0:T(8,128)(2,1)S(1)}, u32[]{:S(2)}, u32[]{:S(2)}) async-start(bf16[8,128,768]{2,1,0:T(8,128)(2,1)} %pad_maximum_fusion.3), calls=%async_computation | async-start | bytes 3145728 | tf_op jit(solution)/shard_map/all_to_all | solution.py:94
  268.7 1.6 copy-start.2
  288.1 25.6 %all-to-all-start.3 = ((bf16[8,128,768]{2,1,0:T(8,128)(2,1)}), bf16[8,128,768]{2,1,0:T(8,128)(2,1)}, u32[]{:S(2)}, u32[]{:S(2)}) async-start(bf16[8,128,768]{2,1,0:T(8,128)(2,1)} %bitcast.23), calls=%async_computation.3 | async-start | bytes 3145728 | tf_op jit(solution)/shard_map/all_to_all | solution.py:102
  313.7 8.3 %copy-start.1 = (bf16[1,2048,768]{2,1,0:T(8,128)(2,1)S(1)}, bf16[1,2048,768]{2,1,0:T(8,128)(2,1)}, u32[]{:S(2)}) copy-start(bf16[1,2048,768]{2,1,0:T(8,128)(2,1)} %param.20) | copy-start | bytes 9437188
Sparse Core Ops, SparseCore 0:
  225.9 41.1 all-gather.1

commit v2 on v1

v2 whole, which is shorter than its diff:
```python
import functools

import jax
import jax.numpy as jnp
from jax import lax
from jax.experimental import pallas as pl
from jax.experimental.pallas import tpu as pltpu
from jax.sharding import PartitionSpec as P

D = 2048
QUERY_HEADS = 32
KEY_VALUE_HEADS = 4
HEAD_SIZE = 128
FFE = 768
TOP = 8
LOG2E = 1.4426950408889634

NN = (((1,), (0,)), ((), ()))
NT = (((1,), (1,)), ((), ()))
TN = (((0,), (0,)), ((), ()))
MESH = pl.DeviceIdType.MESH


def dot(a, b, dims):
    return lax.dot_general(a, b, dims, preferred_element_type=jnp.float32)


def attention_kernel(heads, block, qkv_ref, res_ref, w_ref, out_ref, grad, key_t, dk, dv):
    length = qkv_ref.shape[0]
    width = heads * HEAD_SIZE
    factor = HEAD_SIZE ** (-0.5)
    for lower in range(0, length, block):
        rows = pl.ds(lower, block)
        grad[rows, :] = dot(res_ref[rows, :], w_ref[...], NT).astype(jnp.bfloat16)
    key_t[...] = qkv_ref[:, width : width + HEAD_SIZE].astype(jnp.float32).T.astype(jnp.bfloat16)
    dk[...] = jnp.zeros_like(dk)
    dv[...] = jnp.zeros_like(dv)
    for lower in range(0, length, block):
        rows, upper = pl.ds(lower, block), lower + block
        key_pos = lax.broadcasted_iota(jnp.int32, (block, block), 0)
        query_pos = lax.broadcasted_iota(jnp.int32, (block, block), 1)
        for head in range(heads):
            columns = pl.ds(head * HEAD_SIZE, HEAD_SIZE)
            query, out_grad = qkv_ref[rows, columns], grad[rows, columns]
            keys = qkv_ref[0:upper, width : width + HEAD_SIZE]
            values = qkv_ref[0:upper, width + HEAD_SIZE : width + 2 * HEAD_SIZE]
            scores = dot(keys, query, NT) * (factor * LOG2E)
            last = jnp.where(key_pos <= query_pos, scores[lower:upper], -1e30)
            scores = last if lower == 0 else jnp.concatenate([scores[:lower], last], axis=0)
            exps = jnp.exp2(scores - jnp.max(scores, axis=0, keepdims=True))
            probs = exps * (1.0 / jnp.sum(exps, axis=0, keepdims=True))
            dv[0:upper, :] += dot(probs.astype(jnp.bfloat16), out_grad, NN)
            prob_grad = dot(values, out_grad, NT)
            delta = jnp.sum(probs * prob_grad, axis=0, keepdims=True)
            score_grad = (probs * (prob_grad - delta)).astype(jnp.bfloat16)
            dk[0:upper, :] += dot(score_grad, query, NN)
            query_grad = dot(key_t[:, 0:upper], score_grad, NN) * factor
            out_ref[rows, columns] = query_grad.T.astype(jnp.bfloat16)
    out_ref[:, width : width + HEAD_SIZE] = (dk[...] * factor).astype(jnp.bfloat16)
    out_ref[:, width + HEAD_SIZE : width + 2 * HEAD_SIZE] = dv[...].astype(jnp.bfloat16)


def attention_core(qkv, residual, w_out):
    length, heads = qkv.shape[0], w_out.shape[0] // HEAD_SIZE
    return pl.pallas_call(
        functools.partial(attention_kernel, heads, min(256, length)),
        out_shape=jax.ShapeDtypeStruct(qkv.shape, jnp.bfloat16),
        in_specs=[pl.BlockSpec(memory_space=pltpu.VMEM)] * 3,
        out_specs=pl.BlockSpec(memory_space=pltpu.VMEM),
        scratch_shapes=[
            pltpu.VMEM((length, heads * HEAD_SIZE), jnp.bfloat16),
            pltpu.VMEM((HEAD_SIZE, length), jnp.bfloat16),
            pltpu.VMEM((length, HEAD_SIZE), jnp.float32),
            pltpu.VMEM((length, HEAD_SIZE), jnp.float32),
        ],
        compiler_params=pltpu.CompilerParams(vmem_limit_bytes=48 << 20),
        cost_estimate=pl.CostEstimate(
            flops=9_000_000_000, bytes_accessed=10_000_000, transcendentals=3_000_000
        ),
        name="attention_core",
    )(qkv, residual, w_out)


def return_heads(grads):
    group = lax.axis_size("seq")
    tokens = grads.shape[0] // group
    width = grads.shape[1] - 2 * HEAD_SIZE
    got = lax.all_to_all(
        grads.reshape(group, tokens, -1), "seq", split_axis=0, concat_axis=0, tiled=True
    )
    query_out = jnp.transpose(got[:, :, :width], (1, 0, 2)).reshape(1, tokens, group * width)

    def total(part):
        part = part.astype(jnp.float32).reshape(KEY_VALUE_HEADS, -1, tokens, HEAD_SIZE)
        part = jnp.sum(part, axis=1).astype(jnp.bfloat16)
        return jnp.transpose(part, (1, 0, 2)).reshape(1, tokens, KEY_VALUE_HEADS * HEAD_SIZE)

    return (
        query_out,
        total(got[:, :, width : width + HEAD_SIZE]),
        total(got[:, :, width + HEAD_SIZE :]),
    )


ORDER = 37
GROUP = 32
GROUPS = 4
ROWS = GROUP * 8
PART = ROWS + GROUP
TAIL = D // 8
WIDE = D + FFE
MESSAGE = WIDE + TAIL + HEAD_SIZE


def place_of(order, sign, here):
    x, c, y, z = here
    code = lax.rem(order * ORDER, 128)
    dc, dx, dy, dz = lax.rem(code, 2), lax.rem(code // 2, 4), lax.rem(code // 8, 4), code // 32
    if sign < 0:
        dx, dy, dz = 4 - dx, 4 - dy, 4 - dz
    return (
        lax.rem(x + dx, 4) * 2 + lax.rem(c + dc, 2),
        lax.rem(y + dy, 4) * 4 + lax.rem(z + dz, 4),
    )


def expert_of(order, here):
    seq, expert = place_of(order, 1, here)
    return seq * 16 + expert


def expert_kernel(
    state_ref, gain_ref, layer_ref, grads_ref, routes_ref, gate_hbm, up_hbm, query_hbm, key_hbm,
    value_hbm, residual_ref, gate_out, up_out, query_all, key_all, value_all,
    send, recv, back, back_recv, weights, rows_in, parts, stage, expert_in, hot, hot_t, last,
    codes, last_rows, weight_sem, send_sem, recv_sem, back_sem, back_recv_sem, out_sem,
    head_send, head_recv,
):
    seq, expert = lax.axis_index("seq"), lax.axis_index("expert")
    here = (seq // 2, lax.rem(seq, 2), expert // 4, lax.rem(expert, 4))
    tokens = state_ref.shape[0]
    bf16, f32 = jnp.bfloat16, jnp.float32

    def iota(shape, axis):
        return lax.broadcasted_iota(jnp.int32, shape, axis)

    barrier = pltpu.get_barrier_semaphore()

    def greet(order, carry):
        pl.semaphore_signal(barrier, inc=1, device_id=place_of(order, 1, here), device_id_type=MESH)
        return carry

    lax.fori_loop(1, 128, greet, 0)
    gate_copy = pltpu.make_async_copy(gate_hbm, weights.at[:, pl.ds(0, FFE)], weight_sem.at[0])
    up_copy = pltpu.make_async_copy(up_hbm, weights.at[:, pl.ds(FFE, FFE)], weight_sem.at[1])
    gate_copy.start()
    up_copy.start()

    gain = gain_ref[...].astype(f32)
    state = state_ref[...].astype(f32)
    rstd = lax.rsqrt(jnp.mean(state * state, axis=-1, keepdims=True) + 1e-06)
    expert_in[...] = (state * rstd * gain).astype(bf16)

    lanes = iota((tokens, 128), 1)
    named = [routes_ref[:, k : k + 1] == lanes for k in range(TOP)]
    count = sum(jnp.where(n, 1.0, 0.0) for n in named)
    earlier = jnp.where(iota((tokens, tokens), 0) > iota((tokens, tokens), 1), 1.0, 0.0)
    rank = dot(earlier.astype(bf16), count.astype(bf16), NN)
    columns = iota((tokens, tokens * TOP), 1) - iota((tokens, tokens * TOP), 0) * TOP
    spread_codes = jnp.zeros((tokens, tokens * TOP), f32)
    for k in range(TOP):
        route_rank = jnp.sum(jnp.where(named[k], rank, 0.0), axis=1, keepdims=True)
        code = routes_ref[:, k : k + 1].astype(f32) * 16.0 + route_rank
        spread_codes = jnp.where(columns == k, code, spread_codes)
    codes[...] = jnp.sum(spread_codes, axis=0, keepdims=True)
    target = expert_of(iota((128, 128), 0), here)
    ordered = jnp.where(target == iota((128, 128), 1), 1.0, 0.0).astype(bf16)
    rank_t = dot(ordered, jnp.where(count > 0.0, rank, -1.0).astype(bf16), NT)
    slot = iota((128, 8, tokens), 1).astype(f32)
    rank_wide = jnp.broadcast_to(rank_t[:, None, :], (128, 8, tokens))
    hot_full = jnp.where(rank_wide == slot, 1.0, 0.0).reshape(1024, tokens)
    hot[...] = hot_full.astype(bf16)
    hot_t[:, 0:1024] = hot_full.T.astype(bf16)
    last_full = jnp.where(rank_wide == 8.0, 1.0, 0.0).reshape(1024, tokens)
    hot_t[:, 1024:2048] = last_full.T.astype(bf16)
    last[...] = jnp.where(rank_t == 8.0, 1.0, 0.0).astype(bf16)

    row, col = iota((ROWS, ROWS), 0), iota((ROWS, ROWS), 1)
    spread = jnp.where(col == lax.rem(row, 8) * GROUP + row // 8, 1.0, 0.0).astype(bf16)
    gather = jnp.where(row == lax.rem(col, 8) * GROUP + col // 8, 1.0, 0.0).astype(bf16)

    pl.semaphore_wait(barrier, 127)

    def head_copies(step):
        dx, dc = step // 2, lax.rem(step, 2)
        to = lax.rem(here[0] + dx, 4) * 2 + lax.rem(here[1] + dc, 2)
        rows = pl.ds(pl.multiple_of(seq * tokens, tokens), tokens)
        wide = pl.ds(pl.multiple_of(to * 512, 512), 512)
        narrow = pl.ds(pl.multiple_of(to // 2 * HEAD_SIZE, HEAD_SIZE), HEAD_SIZE)
        return to, (
            (query_hbm.at[:, wide], query_all.at[rows, :]),
            (key_hbm.at[:, narrow], key_all.at[rows, :]),
            (value_hbm.at[:, narrow], value_all.at[rows, :]),
        )

    def head_remote(step):
        to, pairs = head_copies(step)
        return [
            pltpu.make_async_remote_copy(
                src_ref=source, dst_ref=target_ref, send_sem=head_send.at[n, step],
                recv_sem=head_recv.at[n, step], device_id=(to, expert), device_id_type=MESH,
            )
            for n, (source, target_ref) in enumerate(pairs)
        ]

    own = [
        pltpu.make_async_copy(source, target_ref, head_send.at[n, 0])
        for n, (source, target_ref) in enumerate(head_copies(0)[1])
    ]
    for copy in own:
        copy.start()

    def send_heads(step, carry):
        for copy in head_remote(step):
            copy.start()
        return carry

    lax.fori_loop(1, 8, send_heads, 0)

    def dispatch(g, carry):
        at = pl.ds(g * GROUP, GROUP)
        rows = pl.ds(pl.multiple_of(g * ROWS, ROWS), ROWS)
        first = g * GROUP
        x_rows = dot(hot[rows, :], expert_in[...], NN).astype(bf16)
        send[at, :, 0:D] = x_rows.reshape(GROUP, 8, D)
        number = iota((ROWS, 128), 0)
        row_code = (expert_of(first + number // 8, here) * 16 + lax.rem(number, 8)).astype(f32)
        last_code = (expert_of(first + iota((GROUP, 128), 0), here) * 16 + 8).astype(f32)

        def one_hot(code):
            pieces = [
                jnp.where(codes[:, j * 128 : (j + 1) * 128] == code, 1.0, 0.0).astype(bf16)
                for j in range(TOP)
            ]
            return jnp.concatenate(pieces, axis=1)

        h_rows = dot(one_hot(row_code), grads_ref[...], NN).astype(bf16)
        send[at, :, D:WIDE] = h_rows.reshape(GROUP, 8, FFE)
        x_last = dot(last[pl.ds(pl.multiple_of(first, GROUP), GROUP), :], expert_in[...], NN)
        x_last = x_last.astype(bf16)
        h_last = dot(one_hot(last_code), grads_ref[...], NN).astype(bf16)
        x_stack = jnp.concatenate([x_last[:, s * TAIL : (s + 1) * TAIL] for s in range(8)], axis=0)
        h_stack = jnp.concatenate([h_last[:, s * 128 : (s + 1) * 128] for s in range(6)], axis=0)
        x_tail = dot(spread, x_stack, NN).astype(bf16)
        h_tail = dot(spread[:, 0 : 6 * GROUP], h_stack, NN).astype(bf16)
        send[at, :, WIDE : WIDE + TAIL] = x_tail.reshape(GROUP, 8, TAIL)
        send[at, :, WIDE + TAIL : MESSAGE] = h_tail.reshape(GROUP, 8, HEAD_SIZE)

        def start(order, inner):
            pltpu.make_async_remote_copy(
                src_ref=send.at[order], dst_ref=recv.at[order], send_sem=send_sem,
                recv_sem=recv_sem.at[g], device_id=place_of(order, 1, here), device_id_type=MESH,
            ).start()
            return inner

        lax.fori_loop(jnp.maximum(first, 1), first + GROUP, start, 0)
        return carry

    lax.fori_loop(0, GROUPS, dispatch, 0)
    pltpu.make_async_copy(send.at[0], recv.at[0], recv_sem.at[0]).start()
    gate_copy.wait()
    up_copy.wait()

    def work(g, carry):
        at = pl.ds(g * GROUP, GROUP)
        first = g * GROUP
        whole = pl.ds(pl.multiple_of(g * PART, GROUP), PART)
        main = pl.ds(pl.multiple_of(g * PART, GROUP), ROWS)
        tail = pl.ds(pl.multiple_of(g * PART + ROWS, GROUP), GROUP)
        pltpu.make_async_copy(recv.at[at], recv.at[at], recv_sem.at[g]).wait()
        rows_in[main, :] = recv[at, :, 0:D].reshape(ROWS, D)
        x_last = dot(gather, recv[at, :, WIDE : WIDE + TAIL].reshape(ROWS, TAIL), NN).astype(bf16)
        for s in range(8):
            rows_in[tail, s * TAIL : (s + 1) * TAIL] = x_last[s * GROUP : (s + 1) * GROUP, :]
        h_last = dot(
            gather, recv[at, :, WIDE + TAIL : MESSAGE].reshape(ROWS, HEAD_SIZE), NN
        )
        h_last = jnp.concatenate([h_last[s * GROUP : (s + 1) * GROUP, :] for s in range(6)], axis=1)
        for n in range(3):
            tile = slice(n * 256, (n + 1) * 256)
            shifted = slice(FFE + n * 256, FFE + (n + 1) * 256)
            rows_grad = jnp.concatenate(
                [
                    recv[at, :, D + n * 256 : D + (n + 1) * 256].reshape(ROWS, 256).astype(f32),
                    h_last[:, tile],
                ],
                axis=0,
            )
            gate_pre = dot(rows_in[whole, :], weights[:, tile], NN)
            up_pre = dot(rows_in[whole, :], weights[:, shifted], NN)
            sig = jax.nn.sigmoid(gate_pre)
            gate_part = rows_grad * up_pre * sig * (1.0 + gate_pre * (1.0 - sig))
            parts[whole, tile] = gate_part.astype(bf16)
            parts[whole, shifted] = (rows_grad * gate_pre * sig).astype(bf16)

        def back_tile(n, inner):
            source = pl.ds(pl.multiple_of(n * 256, 256), 256)
            rows_back = dot(parts[whole, :], weights[source, :], NT).astype(bf16)
            back[at, :, source] = rows_back[:ROWS, :].reshape(GROUP, 8, 256)
            last_rows[pl.ds(pl.multiple_of(n * GROUP, GROUP), GROUP), :] = rows_back[ROWS:, :]
            return inner

        lax.fori_loop(0, 8, back_tile, 0)
        tails = dot(spread, last_rows[...], NN).astype(bf16)
        back[at, :, D : D + TAIL] = tails.reshape(GROUP, 8, TAIL)

        def start(order, inner):
            pltpu.make_async_remote_copy(
                src_ref=back.at[order], dst_ref=back_recv.at[order], send_sem=back_sem,
                recv_sem=back_recv_sem, device_id=place_of(order, -1, here), device_id_type=MESH,
            ).start()
            return inner

        lax.fori_loop(jnp.maximum(first, 1), first + GROUP, start, 0)
        return carry

    lax.fori_loop(0, GROUPS, work, 0)
    pltpu.make_async_copy(back.at[0], back_recv.at[0], back_recv_sem).start()

    def weight_grads(f, carry):
        tile = pl.ds(pl.multiple_of(f * 256, 256), 256)
        stage[tile, :] = dot(rows_in[:, tile], parts[...], TN).astype(bf16)
        pltpu.make_async_copy(
            stage.at[tile, pl.ds(0, FFE)], gate_out.at[tile, :], out_sem.at[0]
        ).start()
        pltpu.make_async_copy(
            stage.at[tile, pl.ds(FFE, FFE)], up_out.at[tile, :], out_sem.at[1]
        ).start()
        return carry

    lax.fori_loop(0, 8, weight_grads, 0)

    pltpu.make_async_copy(back_recv, back_recv, back_recv_sem).wait()
    slot_of = lax.rem(iota((tokens, 1024), 1), 8)
    state = state_ref[...].astype(f32)
    rstd = lax.rsqrt(jnp.mean(state * state, axis=-1, keepdims=True) + 1e-06)
    inner = jnp.zeros((tokens, 1), f32)
    weighted = []
    for n in range(8):
        tile = slice(n * 256, (n + 1) * 256)
        routed = dot(hot_t[:, 0:1024], back_recv[:, :, tile].reshape(1024, 256), NN)
        chosen = jnp.where(slot_of == n, hot_t[:, 1024:2048], jnp.zeros((), bf16))
        routed += dot(chosen, back_recv[:, :, D : D + TAIL].reshape(1024, TAIL), NN)
        weighted.append(gain[:, tile] * routed)
        inner += jnp.sum(weighted[n] * (state[:, tile] * rstd), axis=-1, keepdims=True)
    inner = inner * (1.0 / D)
    for n in range(8):
        tile = slice(n * 256, (n + 1) * 256)
        change = rstd * (weighted[n] - state[:, tile] * rstd * inner)
        residual_ref[:, tile] = (layer_ref[:, tile].astype(f32) + change).astype(bf16)

    pltpu.make_async_copy(stage.at[:, pl.ds(0, FFE)], gate_out, out_sem.at[0]).wait()
    pltpu.make_async_copy(stage.at[:, pl.ds(FFE, FFE)], up_out, out_sem.at[1]).wait()
    pltpu.make_async_copy(
        send.at[pl.ds(1, 127)], recv.at[pl.ds(1, 127)], send_sem
    ).wait()
    pltpu.make_async_copy(
        back.at[pl.ds(1, 127)], back_recv.at[pl.ds(1, 127)], back_sem
    ).wait()
    for copy in own:
        copy.wait()

    def finish_heads(step, carry):
        for copy in head_remote(step):
            copy.wait()
        return carry

    lax.fori_loop(1, 8, finish_heads, 0)


def expert_block(state, gain, layer_grad, grads, routes, w_gate, w_up, queries, keys, values):
    tokens = state.shape[0]
    bf16, f32 = jnp.bfloat16, jnp.float32
    vmem, hbm = pl.BlockSpec(memory_space=pltpu.VMEM), pl.BlockSpec(memory_space=pl.ANY)
    length = tokens * lax.axis_size("seq")
    dma = pltpu.SemaphoreType.DMA
    return pl.pallas_call(
        expert_kernel,
        out_shape=(
            jax.ShapeDtypeStruct((tokens, D), bf16),
            jax.ShapeDtypeStruct(w_gate.shape, bf16),
            jax.ShapeDtypeStruct(w_up.shape, bf16),
            jax.ShapeDtypeStruct((length, 512), bf16),
            jax.ShapeDtypeStruct((length, HEAD_SIZE), bf16),
            jax.ShapeDtypeStruct((length, HEAD_SIZE), bf16),
        ),
        in_specs=[vmem] * 5 + [hbm] * 5,
        out_specs=(vmem,) + (hbm,) * 5,
        scratch_shapes=[
            pltpu.VMEM((128, 8, MESSAGE), bf16),
            pltpu.VMEM((128, 8, MESSAGE), bf16),
            pltpu.VMEM((128, 8, D + TAIL), bf16),
            pltpu.VMEM((128, 8, D + TAIL), bf16),
            pltpu.VMEM((D, 2 * FFE), bf16),
            pltpu.VMEM((GROUPS * PART, D), bf16),
            pltpu.VMEM((GROUPS * PART, 2 * FFE), bf16),
            pltpu.VMEM((D, 2 * FFE), bf16),
            pltpu.VMEM((tokens, D), bf16),
            pltpu.VMEM((1024, tokens), bf16),
            pltpu.VMEM((tokens, 2048), bf16),
            pltpu.VMEM((128, tokens), bf16),
            pltpu.VMEM((1, tokens * TOP), f32),
            pltpu.VMEM((ROWS, TAIL), bf16),
            dma((2,)),
            dma,
            dma((GROUPS,)),
            dma,
            dma,
            dma((2,)),
            dma((3, 8)),
            dma((3, 8)),
        ],
        compiler_params=pltpu.CompilerParams(
            collective_id=1, has_side_effects=True, vmem_limit_bytes=60 << 20
        ),
        cost_estimate=pl.CostEstimate(
            flops=30_000_000_000, bytes_accessed=20_000_000, transcendentals=1_000_000
        ),
        name="expert_block",
    )(state, gain, layer_grad, grads, routes, w_gate, w_up, queries, keys, values)


def local(
    queries,
    keys,
    values,
    w_out,
    hidden_state,
    norm_gain,
    layer_grad,
    hidden_grad,
    routes,
    w_gate,
    w_up,
):
    residual_rows, gate_grad, up_grad, query_all, key_all, value_all = expert_block(
        hidden_state[0],
        norm_gain[None],
        layer_grad[0],
        hidden_grad[0].reshape(-1, FFE),
        routes[0],
        w_gate[0],
        w_up[0],
        queries[0],
        keys[0],
        values[0],
    )
    qkv = jnp.concatenate([query_all, key_all, value_all], axis=1)
    residual_all = lax.all_gather(residual_rows, "seq", axis=0, tiled=True)
    grads = attention_core(qkv, residual_all, w_out)
    query_out, key_out, value_out = return_heads(grads)
    return (query_out, key_out, value_out, residual_rows[None], gate_grad[None], up_grad[None])


def solution(mesh):
    return jax.shard_map(
        local,
        mesh=mesh,
        in_specs=(
            P("expert", "seq", None),
            P("expert", "seq", None),
            P("expert", "seq", None),
            P("seq", None),
            P("expert", "seq", None),
            P(),
            P("expert", "seq", None),
            P("expert", "seq", None, None),
            P("expert", "seq", None),
            P(("seq", "expert"), None, None),
            P(("seq", "expert"), None, None),
        ),
        out_specs=(
            P("expert", "seq", None),
            P("expert", "seq", None),
            P("expert", "seq", None),
            P("expert", "seq", None),
            P(("seq", "expert"), None, None),
            P(("seq", "expert"), None, None),
        ),
        check_vma=False,
    )
```

time: 335 us -> 274 us (0.82); the launches traced: 329 us -> 274 us
  Pallas kernels: 17.8 us -> 182 us
  blocking collectives: 155 us -> 0 us
  matrix products: 54.6 us -> 0 us
  waiting for transfers between devices: 36.9 us -> 58.1 us
  local copies, waits for them, and re-layouts: 30.1 us -> 14.4 us
  other arithmetic: 10.3 us -> 1.6 us
  starting transfers between devices: 9.78 us -> 3.78 us
    pallas_call x0 -> x1, Pallas kernels: none -> 164 us  [expert_block(): pl.pallas_call(expert_kernel, out_shape=(jax.ShapeDtypeStruct((tokens, D)...]
    all_to_all x2 -> x0, blocking collectives: 155 us -> none  [the longest x1 90.3 us: routed_grads(): lax.all_to_all(send, ('seq', 'expert'), split_axis=0, concat_axis=0, tile...]
    dot_general x13 -> x0, matrix products: 54.6 us -> none  [dot(): return lax.dot_general(a, b, dims, preferred_element_type=jnp.float32)]
    all_gather x1, waiting for transfers between devices: 0.01 us -> 37.4 us  [local(): residual_all = lax.all_gather(residual_rows, 'seq', axis=0, tiled=True)]
    all_to_all x1 -> x0, waiting for transfers between devices: 26 us -> none  [exchange_heads(): got = lax.all_to_all(send, 'seq', split_axis=0, concat_axis=0, tiled=True)]
    all_to_all x1, waiting for transfers between devices: 10.9 us -> 20.7 us  [return_heads(): lax.all_to_all(grads.reshape(group, tokens, -1), 'seq', split_axis=0, con...]
    reshape x4 -> x0, local copies, waits for them, and re-layouts: 6.88 us -> none  [the longest x1 2.82 us: routed_grads(): got[:, :, :D].reshape(devices * 8, D)]
    all_to_all x1 -> x0, starting transfers between devices: 4.99 us -> none  [exchange_heads(): got = lax.all_to_all(send, 'seq', split_axis=0, concat_axis=0, tiled=True)]
  transfers between devices with their start and end apart: 3 -> 2, of which waited for: 2 -> 2; matrix products, arithmetic and copies ran while one was open for 7% -> 1% of each run, Pallas kernels for 0% -> 0%
where the time goes in v2:
time: 274 us
  Pallas kernels  182 us (66%)
  waiting for transfers between devices  58.1 us (21%)
  local copies, waits for them, and re-layouts  14.4 us (5%)
  between operations  14.1 us (5%)
  starting transfers between devices  3.78 us (1%)
    pallas_call x1, Pallas kernels, expert_block(): pl.pallas_call(expert_kernel, out_shape=(jax.ShapeDtypeStruct((tokens, D)...  164 us
    all_gather x1, waiting for transfers between devices, local(): residual_all = lax.all_gather(residual_rows, 'seq', axis=0, tiled=True)  37.4 us
    all_to_all x1, waiting for transfers between devices, return_heads(): lax.all_to_all(grads.reshape(group, tokens, -1), 'seq', split_axis=0, con...  20.7 us
    pallas_call x1, Pallas kernels, attention_core(): pl.pallas_call(functools.partial(attention_kernel, heads, min(256, length...  17.8 us
    unnamed x12, local copies, waits for them, and re-layouts  10.9 us
  transfers between devices with their start and end apart: 2, of which 2 were waited for; matrix products, arithmetic and copies ran while one was open for 1% of the time, Pallas kernels for 0%

profile of v2, /device:TPU:1, one launch (start us, length us, event | category | flops | bytes accessed | tf_op | source)
XLA Modules:
  0.0 274.0 jit_solution(16682780648168799701)
XLA Ops:
  7.2 0.0 all-gather.2.cloned.1.call-start
  7.2 1.3 broadcast_in_dim.12.gain_ref
  8.5 1.4 copy.21
  9.9 164.1 %expert_block.1 = (bf16[128,2048]{1,0:T(8,128)(2,1)}, bf16[2048,768]{1,0:T(8,128)(2,1)}, bf16[2048,768]{1,0:T(8,128)(2,1)}, bf16[1024,512]{1,0:T(8,128)(2,1)}, b...) custom-call(bf16[128,2048]{1,0:T(8,128)(2,1)} %bitcast.35, bf16[1,2048]{1,0:T(2,128)(2,1)} %broadcast_in_dim.12.gain_ref, ...), custom_call_target="tpu_custom_call" | custom-call | flops 30000001024 | bytes 20000000 | tf_op jit(solution)/shard_map/expert_block/pallas_call | solution.py:387
  174.1 0.0 all-gather.2.cloned.1.call-update
  174.1 1.5 pad_maximum_fusion.qkv_ref
  175.6 37.4 %all-gather.2.cloned.1.call-done.res_ref = bf16[1024,2048]{1,0:T(8,128)(2,1)} async-done(((bf16[128,2048]{1,0:T(8,128)(2,1)}), bf16[1024,2048]{1,0:T(8,128)(2,1)}) %all-gather.2.cloned.1.call-update) | async-done | bytes 4194320 | tf_op jit(solution)/shard_map/all_gather | solution.py:459
  213.0 0.0 copy-start
  213.0 1.6 copy-done
  214.6 17.8 %attention_core.1 = bf16[1024,768]{1,0:T(8,128)(2,1)} custom-call(bf16[1024,768]{1,0:T(8,128)(2,1)S(1)} %pad_maximum_fusion.qkv_ref, bf16[1024,2048]{1,0:T(8,128)(2,1)} %all-gather.2.cloned.1.call-done.res_ref, bf16[512,2048]{1,0:T(8,128)(2,1)S(1)} %copy-done), custom_call_target="tpu_custom_call" | custom-call | flops 8999999488 | bytes 10000000 | tf_op jit(solution)/shard_map/attention_core/pallas_call | solution.py:65
  232.4 3.7 %all-to-all-start = ((bf16[8,128,768]{2,1,0:T(8,128)(2,1)}), bf16[8,128,768]{2,1,0:T(8,128)(2,1)S(1)}, u32[]{:S(2)}, u32[]{:S(2)}) async-start(bf16[8,128,768]{2,1,0:T(8,128)(2,1)} %bitcast.9), calls=%async_computation | async-start | bytes 3145728 | tf_op jit(solution)/shard_map/all_to_all | solution.py:88
  236.2 20.7 %all-to-all-done = bf16[8,128,768]{2,1,0:T(8,128)(2,1)S(1)} async-done(((bf16[8,128,768]{2,1,0:T(8,128)(2,1)}), bf16[8,128,768]{2,1,0:T(8,128)(2,1)S(1)}, u32[]{:S(2)}, u32[]{:S(2)}) %all-to-all-start) | async-done | bytes 1572896 | tf_op jit(solution)/shard_map/all_to_all | solution.py:88
  256.9 0.1 slice_bitcast_fusion
  257.0 0.0 copy-start.2
  257.0 0.6 copy.22
  257.6 1.3 reshape.37
  258.9 0.1 bitcast_reduce_fusion
  259.0 0.1 copy.24
  259.1 0.8 copy.26
  259.9 0.1 copy.23
  260.0 0.8 copy.25
  260.8 0.0 copy-done.2
  260.8 0.8 copy.30
  261.6 0.0 copy-start.1
  261.6 3.9 %copy.31 = bf16[1,2048,768]{2,1,0:T(8,128)(2,1)} copy(bf16[1,2048,768]{2,1,0:T(8,128)(2,1)} %bitcast.24) | data formatting | bytes 6291456
  265.5 0.0 copy-done.1
  265.5 1.7 copy.32
Async XLA Ops:
  7.2 205.8 %all-gather.2.cloned.1.call-start = ((), (), s32[]{:S(2)}) async-start(), calls=%async_computation.1 | async-start | bytes 4718592 | tf_op jit(solution)/shard_map/all_gather | solution.py:459
  213.0 1.6 copy-start
  232.4 24.5 %all-to-all-start = ((bf16[8,128,768]{2,1,0:T(8,128)(2,1)}), bf16[8,128,768]{2,1,0:T(8,128)(2,1)S(1)}, u32[]{:S(2)}, u32[]{:S(2)}) async-start(bf16[8,128,768]{2,1,0:T(8,128)(2,1)} %bitcast.9), calls=%async_computation | async-start | bytes 3145728 | tf_op jit(solution)/shard_map/all_to_all | solution.py:88
  257.0 3.8 %copy-start.2 = (bf16[128,2048]{1,0:T(8,128)(2,1)S(1)}, bf16[128,2048]{1,0:T(8,128)(2,1)}, u32[]{:S(2)}) copy-start(bf16[128,2048]{1,0:T(8,128)(2,1)} %get-tuple-element.15) | copy-start | bytes 1572868
  261.6 3.9 %copy-start.1 = (bf16[2048,768]{1,0:T(8,128)(2,1)S(1)}, bf16[2048,768]{1,0:T(8,128)(2,1)}, u32[]{:S(2)}) copy-start(bf16[2048,768]{1,0:T(8,128)(2,1)} %get-tuple-element.17) | copy-start | bytes 9437188
Sparse Core Ops, SparseCore 0:
  174.2 38.7 all-gather.1

commit v3 on v2

--- a/solution.py
+++ b/solution.py
@@ -25,81 +25,249 @@
     return lax.dot_general(a, b, dims, preferred_element_type=jnp.float32)
 
 
-def attention_kernel(heads, block, qkv_ref, res_ref, w_ref, out_ref, grad, key_t, dk, dv):
-    length = qkv_ref.shape[0]
-    width = heads * HEAD_SIZE
+def attention_kernel(
+    residual_ref, w_hbm, query_hbm, key_hbm, value_hbm, query_out, key_out, value_out,
+    gathered, w_out, queries, keys, values, grad, key_t, dk, dv, packed, returned,
+    probs_0, probs_1, probs_2, probs_3, load_sem, gather_send, gather_recv,
+    query_send, query_recv, pair_send, pair_recv,
+):
+    seq, expert = lax.axis_index("seq"), lax.axis_index("expert")
+    x, c = seq // 2, lax.rem(seq, 2)
+    tokens = residual_ref.shape[0]
+    half = tokens // 2
+    bf16, f32 = jnp.bfloat16, jnp.float32
     factor = HEAD_SIZE ** (-0.5)
-    for lower in range(0, length, block):
-        rows = pl.ds(lower, block)
-        grad[rows, :] = dot(res_ref[rows, :], w_ref[...], NT).astype(jnp.bfloat16)
-    key_t[...] = qkv_ref[:, width : width + HEAD_SIZE].astype(jnp.float32).T.astype(jnp.bfloat16)
+    probs = (probs_0, probs_1, probs_2, probs_3)
+    block = 2 * tokens
+
+    def device(dx, dc):
+        return lax.rem(x + dx, 4) * 2 + lax.rem(c + dc, 2)
+
+    barrier = pltpu.get_barrier_semaphore()
+    for step in range(1, 8):
+        pl.semaphore_signal(
+            barrier, inc=1, device_id=(device(step // 2, step % 2), expert), device_id_type=MESH
+        )
+    loads = [
+        pltpu.make_async_copy(source, target, load_sem.at[n])
+        for n, (source, target) in enumerate(
+            ((query_hbm, queries), (key_hbm, keys), (value_hbm, values), (w_hbm, w_out))
+        )
+    ]
+    for load in loads:
+        load.start()
+
+    def rows_of(owner, start, size):
+        return pl.ds(pl.multiple_of(owner * tokens + start, size), size)
+
+    def gather_copy(number, owner, start, size, to):
+        rows = rows_of(owner, start, size)
+        return pltpu.make_async_remote_copy(
+            src_ref=gathered.at[rows, :], dst_ref=gathered.at[rows, :],
+            send_sem=gather_send.at[number], recv_sem=gather_recv.at[number],
+            device_id=(to, expert), device_id_type=MESH,
+        )
+
+    own, left, right, far = device(0, 0), device(3, 0), device(1, 0), device(2, 0)
+    mate = device(0, 1)
+    gathered[rows_of(own, 0, tokens), :] = residual_ref[...]
+    pl.semaphore_wait(barrier, 7)
+    copies = [
+        gather_copy(0, own, 0, half, right),
+        gather_copy(1, own, half, half, left),
+        gather_copy(2, own, half, half, right),
+        gather_copy(3, own, 0, half, left),
+        gather_copy(4, own, 0, tokens, mate),
+        gather_copy(5, left, 0, half, right),
+        gather_copy(6, right, half, half, left),
+        gather_copy(7, left, 0, half, mate),
+        gather_copy(8, right, half, half, mate),
+        gather_copy(9, left, half, half, mate),
+        gather_copy(10, right, 0, half, mate),
+        gather_copy(11, far, 0, half, mate),
+        gather_copy(12, far, half, half, mate),
+    ]
+    for copy in copies[:5]:
+        copy.start()
+    for load in loads:
+        load.wait()
+
+    key_t[...] = keys[...].astype(f32).T.astype(bf16)
     dk[...] = jnp.zeros_like(dk)
     dv[...] = jnp.zeros_like(dv)
-    for lower in range(0, length, block):
-        rows, upper = pl.ds(lower, block), lower + block
+
+    def softmax_block(i):
+        lower, upper = i * block, (i + 1) * block
         key_pos = lax.broadcasted_iota(jnp.int32, (block, block), 0)
         query_pos = lax.broadcasted_iota(jnp.int32, (block, block), 1)
-        for head in range(heads):
-            columns = pl.ds(head * HEAD_SIZE, HEAD_SIZE)
-            query, out_grad = qkv_ref[rows, columns], grad[rows, columns]
-            keys = qkv_ref[0:upper, width : width + HEAD_SIZE]
-            values = qkv_ref[0:upper, width + HEAD_SIZE : width + 2 * HEAD_SIZE]
-            scores = dot(keys, query, NT) * (factor * LOG2E)
-            last = jnp.where(key_pos <= query_pos, scores[lower:upper], -1e30)
-            scores = last if lower == 0 else jnp.concatenate([scores[:lower], last], axis=0)
+        for head in range(4):
+            columns = slice(head * HEAD_SIZE, (head + 1) * HEAD_SIZE)
+            scores = dot(keys[0:upper, :], queries[lower:upper, columns], NT) * (factor * LOG2E)
+            diagonal = jnp.where(key_pos <= query_pos, scores[lower:upper], -1e30)
+            scores = diagonal if i == 0 else jnp.concatenate([scores[:lower], diagonal], axis=0)
             exps = jnp.exp2(scores - jnp.max(scores, axis=0, keepdims=True))
-            probs = exps * (1.0 / jnp.sum(exps, axis=0, keepdims=True))
-            dv[0:upper, :] += dot(probs.astype(jnp.bfloat16), out_grad, NN)
-            prob_grad = dot(values, out_grad, NT)
-            delta = jnp.sum(probs * prob_grad, axis=0, keepdims=True)
-            score_grad = (probs * (prob_grad - delta)).astype(jnp.bfloat16)
-            dk[0:upper, :] += dot(score_grad, query, NN)
+            probs[i][head, :, :] = exps * (1.0 / jnp.sum(exps, axis=0, keepdims=True))
+
+    def project(owner):
+        rows = rows_of(owner, 0, tokens)
+        grad[rows, :] = dot(gathered[rows, :], w_out[...], NT).astype(bf16)
+
+    softmax_block(0)
+    softmax_block(1)
+    copies[0].wait_recv()
+    copies[5].start()
+    copies[7].start()
+    copies[1].wait_recv()
+    copies[6].start()
+    copies[8].start()
+    softmax_block(2)
+    copies[2].wait_recv()
+    copies[9].start()
+    copies[3].wait_recv()
+    copies[10].start()
+    softmax_block(3)
+    project(own)
+    copies[4].wait_recv()
+    project(mate)
+    project(left)
+    project(right)
+    copies[5].wait_recv()
+    copies[11].start()
+    copies[6].wait_recv()
+    copies[12].start()
+    project(far)
+    for copy in copies[7:11]:
+        copy.wait_recv()
+    project(device(3, 1))
+    project(device(1, 1))
+    for copy in copies[11:]:
+        copy.wait_recv()
+    project(device(2, 1))
+
+    def backward_block(i):
+        lower, upper = i * block, (i + 1) * block
+        for head in range(4):
+            columns = slice(head * HEAD_SIZE, (head + 1) * HEAD_SIZE)
+            out_grad = grad[lower:upper, columns]
+            prob = probs[i][head]
+            dv[0:upper, :] += dot(prob.astype(bf16), out_grad, NN)
+            prob_grad = dot(values[0:upper, :], out_grad, NT)
+            delta = jnp.sum(prob * prob_grad, axis=0, keepdims=True)
+            score_grad = (prob * (prob_grad - delta)).astype(bf16)
+            dk[0:upper, :] += dot(score_grad, queries[lower:upper, columns], NN)
             query_grad = dot(key_t[:, 0:upper], score_grad, NN) * factor
-            out_ref[rows, columns] = query_grad.T.astype(jnp.bfloat16)
-    out_ref[:, width : width + HEAD_SIZE] = (dk[...] * factor).astype(jnp.bfloat16)
-    out_ref[:, width + HEAD_SIZE : width + 2 * HEAD_SIZE] = dv[...].astype(jnp.bfloat16)
-
-
-def attention_core(qkv, residual, w_out):
-    length, heads = qkv.shape[0], w_out.shape[0] // HEAD_SIZE
+            packed[lower:upper, columns] = query_grad.T.astype(bf16)
+
+    pair = slice(4 * HEAD_SIZE, 6 * HEAD_SIZE)
+
+    def query_copy(dx, dc):
+        to, number = device(dx, dc), dx * 2 + dc
+        return pltpu.make_async_remote_copy(
+            src_ref=packed.at[rows_of(to, 0, tokens), pl.ds(0, 512)],
+            dst_ref=query_out.at[:, pl.ds(pl.multiple_of(seq * 512, 512), 512)],
+            send_sem=query_send.at[number], recv_sem=query_recv.at[number],
+            device_id=(to, expert), device_id_type=MESH,
+        )
+
+    def pair_copy(dx, dc):
+        to, number = device(dx, dc), dx * 2 + dc
+        return pltpu.make_async_remote_copy(
+            src_ref=packed.at[rows_of(to, 0, tokens), pl.ds(512, 256)],
+            dst_ref=returned.at[seq],
+            send_sem=pair_send.at[number], recv_sem=pair_recv.at[number],
+            device_id=(to, expert), device_id_type=MESH,
+        )
+
+    own_query = pltpu.make_async_copy(
+        packed.at[rows_of(seq, 0, tokens), pl.ds(0, 512)],
+        query_out.at[:, pl.ds(pl.multiple_of(seq * 512, 512), 512)],
+        query_send.at[0],
+    )
+
+    def backward_step(step, carry):
+        dx = lax.rem(step + 1, 4)
+        chip = lax.rem(x + dx, 4)
+        for i in range(4):
+            pl.when(chip == i)(functools.partial(backward_block, i))
+
+        @pl.when(step < 3)
+        def _():
+            query_copy(dx, 0).start()
+
+        @pl.when(step == 3)
+        def _():
+            own_query.start()
+
+        query_copy(dx, 1).start()
+        return carry
+
+    lax.fori_loop(0, 4, backward_step, 0)
+    packed[:, 512:640] = (dk[...] * factor).astype(bf16)
+    packed[:, 640:768] = dv[...].astype(bf16)
+    for step in (2, 3, 4, 5, 6, 7, 1):
+        pair_copy(step // 2, step % 2).start()
+    returned[seq, :, :] = packed[rows_of(seq, 0, tokens), pair]
+    for step in range(1, 8):
+        pair_copy(step // 2, step % 2).wait_recv()
+    for head in range(KEY_VALUE_HEADS):
+        total = returned[2 * head].astype(f32) + returned[2 * head + 1].astype(f32)
+        columns = slice(head * HEAD_SIZE, (head + 1) * HEAD_SIZE)
+        key_out[:, columns] = total[:, 0:HEAD_SIZE].astype(bf16)
+        value_out[:, columns] = total[:, HEAD_SIZE:].astype(bf16)
+    for copy in copies:
+        copy.wait_send()
+    for step in range(1, 8):
+        query_copy(step // 2, step % 2).wait()
+        pair_copy(step // 2, step % 2).wait_send()
+    own_query.wait()
+
+
+def attention_core(residual, w_out, queries, keys, values):
+    tokens, length = residual.shape[0], queries.shape[0]
+    bf16, f32 = jnp.bfloat16, jnp.float32
+    vmem, hbm = pl.BlockSpec(memory_space=pltpu.VMEM), pl.BlockSpec(memory_space=pl.ANY)
+    dma = pltpu.SemaphoreType.DMA
     return pl.pallas_call(
-        functools.partial(attention_kernel, heads, min(256, length)),
-        out_shape=jax.ShapeDtypeStruct(qkv.shape, jnp.bfloat16),
-        in_specs=[pl.BlockSpec(memory_space=pltpu.VMEM)] * 3,
-        out_specs=pl.BlockSpec(memory_space=pltpu.VMEM),
+        attention_kernel,
+        out_shape=(
+            jax.ShapeDtypeStruct((tokens, QUERY_HEADS * HEAD_SIZE), bf16),
+            jax.ShapeDtypeStruct((tokens, KEY_VALUE_HEADS * HEAD_SIZE), bf16),
+            jax.ShapeDtypeStruct((tokens, KEY_VALUE_HEADS * HEAD_SIZE), bf16),
+        ),
+        in_specs=[vmem] + [hbm] * 4,
+        out_specs=(hbm, vmem, vmem),
         scratch_shapes=[
-            pltpu.VMEM((length, heads * HEAD_SIZE), jnp.bfloat16),
-            pltpu.VMEM((HEAD_SIZE, length), jnp.bfloat16),
-            pltpu.VMEM((length, HEAD_SIZE), jnp.float32),
-            pltpu.VMEM((length, HEAD_SIZE), jnp.float32),
+            pltpu.VMEM((length, D), bf16),
+            pltpu.VMEM(w_out.shape, bf16),
+            pltpu.VMEM(queries.shape, bf16),
+            pltpu.VMEM(keys.shape, bf16),
+            pltpu.VMEM(values.shape, bf16),
+            pltpu.VMEM((length, 512), bf16),
+            pltpu.VMEM((HEAD_SIZE, length), bf16),
+            pltpu.VMEM((length, HEAD_SIZE), f32),
+            pltpu.VMEM((length, HEAD_SIZE), f32),
+            pltpu.VMEM((length, 768), bf16),
+            pltpu.VMEM((8, tokens, 256), bf16),
+            pltpu.VMEM((4, 256, 256), f32),
+            pltpu.VMEM((4, 512, 256), f32),
+            pltpu.VMEM((4, 768, 256), f32),
+            pltpu.VMEM((4, 1024, 256), f32),
+            dma((4,)),
+            dma((13,)),
+            dma((13,)),
+            dma((8,)),
+            dma((8,)),
+            dma((8,)),
+            dma((8,)),
         ],
-        compiler_params=pltpu.CompilerParams(vmem_limit_bytes=48 << 20),
+        compiler_params=pltpu.CompilerParams(
+            collective_id=2, has_side_effects=True, vmem_limit_bytes=56 << 20
+        ),
         cost_estimate=pl.CostEstimate(
             flops=9_000_000_000, bytes_accessed=10_000_000, transcendentals=3_000_000
         ),
         name="attention_core",
-    )(qkv, residual, w_out)
-
-
-def return_heads(grads):
-    group = lax.axis_size("seq")
-    tokens = grads.shape[0] // group
-    width = grads.shape[1] - 2 * HEAD_SIZE
-    got = lax.all_to_all(
-        grads.reshape(group, tokens, -1), "seq", split_axis=0, concat_axis=0, tiled=True
-    )
-    query_out = jnp.transpose(got[:, :, :width], (1, 0, 2)).reshape(1, tokens, group * width)
-
-    def total(part):
-        part = part.astype(jnp.float32).reshape(KEY_VALUE_HEADS, -1, tokens, HEAD_SIZE)
-        part = jnp.sum(part, axis=1).astype(jnp.bfloat16)
-        return jnp.transpose(part, (1, 0, 2)).reshape(1, tokens, KEY_VALUE_HEADS * HEAD_SIZE)
-
-    return (
-        query_out,
-        total(got[:, :, width : width + HEAD_SIZE]),
-        total(got[:, :, width + HEAD_SIZE :]),
-    )
+    )(residual, w_out, queries, keys, values)
 
 
 ORDER = 37
@@ -157,12 +325,14 @@
     up_copy.start()
 
     gain = gain_ref[...].astype(f32)
+    gain = jnp.concatenate([gain[j : j + 1, :] for j in range(D // 128)], axis=1)
     state = state_ref[...].astype(f32)
     rstd = lax.rsqrt(jnp.mean(state * state, axis=-1, keepdims=True) + 1e-06)
     expert_in[...] = (state * rstd * gain).astype(bf16)
 
     lanes = iota((tokens, 128), 1)
-    named = [routes_ref[:, k : k + 1] == lanes for k in range(TOP)]
+    route = routes_ref[...].astype(f32).T
+    named = [route[:, k : k + 1] == lanes.astype(f32) for k in range(TOP)]
     count = sum(jnp.where(n, 1.0, 0.0) for n in named)
     earlier = jnp.where(iota((tokens, tokens), 0) > iota((tokens, tokens), 1), 1.0, 0.0)
     rank = dot(earlier.astype(bf16), count.astype(bf16), NN)
@@ -170,7 +340,7 @@
     spread_codes = jnp.zeros((tokens, tokens * TOP), f32)
     for k in range(TOP):
         route_rank = jnp.sum(jnp.where(named[k], rank, 0.0), axis=1, keepdims=True)
-        code = routes_ref[:, k : k + 1].astype(f32) * 16.0 + route_rank
+        code = route[:, k : k + 1] * 16.0 + route_rank
         spread_codes = jnp.where(columns == k, code, spread_codes)
     codes[...] = jnp.sum(spread_codes, axis=0, keepdims=True)
     target = expert_of(iota((128, 128), 0), here)
@@ -445,21 +615,20 @@
 ):
     residual_rows, gate_grad, up_grad, query_all, key_all, value_all = expert_block(
         hidden_state[0],
-        norm_gain[None],
+        norm_gain.reshape(D // 128, 128),
         layer_grad[0],
         hidden_grad[0].reshape(-1, FFE),
-        routes[0],
+        routes[0].T,
         w_gate[0],
         w_up[0],
         queries[0],
         keys[0],
         values[0],
     )
-    qkv = jnp.concatenate([query_all, key_all, value_all], axis=1)
-    residual_all = lax.all_gather(residual_rows, "seq", axis=0, tiled=True)
-    grads = attention_core(qkv, residual_all, w_out)
-    query_out, key_out, value_out = return_heads(grads)
-    return (query_out, key_out, value_out, residual_rows[None], gate_grad[None], up_grad[None])
+    query_out, key_out, value_out = attention_core(
+        residual_rows, w_out, query_all, key_all, value_all
+    )
+    return (query_out[None], key_out[None], value_out[None], residual_rows[None], gate_grad[None], up_grad[None])
 
 
 def solution(mesh):

time: 274 us -> 232 us (0.85); the launches traced: 274 us -> 229 us
  waiting for transfers between devices: 58.1 us -> 0 us
  Pallas kernels: 182 us -> 217 us
  between operations: 14.1 us -> 0.67 us
  starting transfers between devices: 3.78 us -> 0 us
  local copies, waits for them, and re-layouts: 14.4 us -> 11.1 us
    all_gather x1 -> x0, waiting for transfers between devices: 37.4 us -> none  [local(): residual_all = lax.all_gather(residual_rows, 'seq', axis=0, tiled=True)]
    pallas_call x1, Pallas kernels: 17.8 us -> 50.4 us  [attention_core(): pl.pallas_call(attention_kernel, out_shape=(jax.ShapeDtypeStruct((tokens,...]
    all_to_all x1 -> x0, waiting for transfers between devices: 20.7 us -> none  [return_heads(): lax.all_to_all(grads.reshape(group, tokens, -1), 'seq', split_axis=0, con...]
    all_to_all x1 -> x0, starting transfers between devices: 3.74 us -> none  [return_heads(): lax.all_to_all(grads.reshape(group, tokens, -1), 'seq', split_axis=0, con...]
  transfers between devices with their start and end apart: 2 -> 0, of which waited for: 2 -> 0; matrix products, arithmetic and copies ran while one was open for 1% -> 0% of each run, Pallas kernels for 0% -> 0%
where the time goes in v3:
time: 232 us; the launch traced here: 229 us
  Pallas kernels  217 us (94%)
  local copies, waits for them, and re-layouts  11.1 us (5%)
    pallas_call x1, Pallas kernels, expert_block(): pl.pallas_call(expert_kernel, out_shape=(jax.ShapeDtypeStruct((tokens, D)...  166 us
    pallas_call x1, Pallas kernels, attention_core(): pl.pallas_call(attention_kernel, out_shape=(jax.ShapeDtypeStruct((tokens,...  50.4 us
    unnamed x12, local copies, waits for them, and re-layouts  11.1 us

profile of v3, /device:TPU:1, one launch (start us, length us, event | category | flops | bytes accessed | tf_op | source)
XLA Modules:
  0.0 228.5 jit_solution(7386466647847831550)
XLA Ops:
  0.6 166.4 %expert_block.1 = (bf16[128,2048]{1,0:T(8,128)(2,1)}, bf16[2048,768]{1,0:T(8,128)(2,1)}, bf16[2048,768]{1,0:T(8,128)(2,1)}, bf16[1024,512]{1,0:T(8,128)(2,1)}, b...) custom-call(bf16[128,2048]{1,0:T(8,128)(2,1)} %bitcast.28, bf16[16,128]{1,0:T(8,128)(2,1)} %bitcast.32, ...), custom_call_target="tpu_custom_call" | custom-call | flops 30000001024 | bytes 20000000 | tf_op jit(solution)/shard_map/expert_block/pallas_call | solution.py:557
  167.0 0.0 copy-start.2
  167.0 50.4 %attention_core.1 = (bf16[128,4096]{1,0:T(8,128)(2,1)}, bf16[128,512]{1,0:T(8,128)(2,1)}, bf16[128,512]{1,0:T(8,128)(2,1)}) custom-call(bf16[128,2048]{1,0:T(8,128)(2,1)} %get-tuple-element.15.residual_ref, bf16[512,2048]{1,0:T(8,128)(2,1)} %w_hbm.1, bf16[1024,512]{1,0:T(8,128)(2,1)} %get-tuple-element.16.query_hbm, ...), custom_call_target="tpu_custom_call" | custom-call | flops 8999999488 | bytes 10000000 | tf_op jit(solution)/shard_map/attention_core/pallas_call | solution.py:230
  217.5 0.0 copy-start.1
  217.5 2.4 %copy.23 = bf16[1,128,4096]{2,1,0:T(8,128)(2,1)} copy(bf16[1,128,4096]{2,1,0:T(8,128)(2,1)} %bitcast.20) | data formatting | bytes 2097152
  219.9 1.6 copy.24
  221.5 1.6 copy.25
  223.1 0.0 copy-done.2
  223.1 0.8 copy.26
  223.9 0.0 copy-done.1
  223.9 0.0 copy-start
  223.9 1.7 copy.27
  225.5 1.4 copy-done
  226.9 1.7 copy.28
Async XLA Ops:
  167.0 56.0 %copy-start.2 = (bf16[128,2048]{1,0:T(8,128)(2,1)S(1)}, bf16[128,2048]{1,0:T(8,128)(2,1)}, u32[]{:S(2)}) copy-start(bf16[128,2048]{1,0:T(8,128)(2,1)} %get-tuple-element.15.residual_ref) | copy-start | bytes 1572868
  217.5 6.4 %copy-start.1 = (bf16[2048,768]{1,0:T(8,128)(2,1)S(1)}, bf16[2048,768]{1,0:T(8,128)(2,1)}, u32[]{:S(2)}) copy-start(bf16[2048,768]{1,0:T(8,128)(2,1)} %get-tuple-element.22) | copy-start | bytes 9437188
  223.9 3.0 %copy-start = (bf16[2048,768]{1,0:T(8,128)(2,1)S(1)}, bf16[2048,768]{1,0:T(8,128)(2,1)}, u32[]{:S(2)}) copy-start(bf16[2048,768]{1,0:T(8,128)(2,1)} %get-tuple-element.23) | copy-start | bytes 9437188

commit v4 on v3

--- a/solution.py
+++ b/solution.py
@@ -270,7 +270,7 @@
     )(residual, w_out, queries, keys, values)
 
 
-ORDER = 37
+ORDER = 101
 GROUP = 32
 GROUPS = 4
 ROWS = GROUP * 8
@@ -306,6 +306,7 @@
 ):
     seq, expert = lax.axis_index("seq"), lax.axis_index("expert")
     here = (seq // 2, lax.rem(seq, 2), expert // 4, lax.rem(expert, 4))
+    turn = seq * 13 + expert * 7
     tokens = state_ref.shape[0]
     bf16, f32 = jnp.bfloat16, jnp.float32
 
@@ -329,6 +330,44 @@
     state = state_ref[...].astype(f32)
     rstd = lax.rsqrt(jnp.mean(state * state, axis=-1, keepdims=True) + 1e-06)
     expert_in[...] = (state * rstd * gain).astype(bf16)
+
+    pl.semaphore_wait(barrier, 127)
+
+    def head_copies(step):
+        dx, dc = step // 2, lax.rem(step, 2)
+        to = lax.rem(here[0] + dx, 4) * 2 + lax.rem(here[1] + dc, 2)
+        rows = pl.ds(pl.multiple_of(seq * tokens, tokens), tokens)
+        wide = pl.ds(pl.multiple_of(to * 512, 512), 512)
+        narrow = pl.ds(pl.multiple_of(to // 2 * HEAD_SIZE, HEAD_SIZE), HEAD_SIZE)
+        return to, (
+            (query_hbm.at[:, wide], query_all.at[rows, :]),
+            (key_hbm.at[:, narrow], key_all.at[rows, :]),
+            (value_hbm.at[:, narrow], value_all.at[rows, :]),
+        )
+
+    def head_remote(step):
+        to, pairs = head_copies(step)
+        return [
+            pltpu.make_async_remote_copy(
+                src_ref=source, dst_ref=target_ref, send_sem=head_send.at[n, step],
+                recv_sem=head_recv.at[n, step], device_id=(to, expert), device_id_type=MESH,
+            )
+            for n, (source, target_ref) in enumerate(pairs)
+        ]
+
+    own = [
+        pltpu.make_async_copy(source, target_ref, head_send.at[n, 0])
+        for n, (source, target_ref) in enumerate(head_copies(0)[1])
+    ]
+    for copy in own:
+        copy.start()
+
+    def send_heads(step, carry):
+        for copy in head_remote(step):
+            copy.start()
+        return carry
+
+    lax.fori_loop(1, 8, send_heads, 0)
 
     lanes = iota((tokens, 128), 1)
     route = routes_ref[...].astype(f32).T
@@ -359,44 +398,6 @@
     spread = jnp.where(col == lax.rem(row, 8) * GROUP + row // 8, 1.0, 0.0).astype(bf16)
     gather = jnp.where(row == lax.rem(col, 8) * GROUP + col // 8, 1.0, 0.0).astype(bf16)
 
-    pl.semaphore_wait(barrier, 127)
-
-    def head_copies(step):
-        dx, dc = step // 2, lax.rem(step, 2)
-        to = lax.rem(here[0] + dx, 4) * 2 + lax.rem(here[1] + dc, 2)
-        rows = pl.ds(pl.multiple_of(seq * tokens, tokens), tokens)
-        wide = pl.ds(pl.multiple_of(to * 512, 512), 512)
-        narrow = pl.ds(pl.multiple_of(to // 2 * HEAD_SIZE, HEAD_SIZE), HEAD_SIZE)
-        return to, (
-            (query_hbm.at[:, wide], query_all.at[rows, :]),
-            (key_hbm.at[:, narrow], key_all.at[rows, :]),
-            (value_hbm.at[:, narrow], value_all.at[rows, :]),
-        )
-
-    def head_remote(step):
-        to, pairs = head_copies(step)
-        return [
-            pltpu.make_async_remote_copy(
-                src_ref=source, dst_ref=target_ref, send_sem=head_send.at[n, step],
-                recv_sem=head_recv.at[n, step], device_id=(to, expert), device_id_type=MESH,
-            )
-            for n, (source, target_ref) in enumerate(pairs)
-        ]
-
-    own = [
-        pltpu.make_async_copy(source, target_ref, head_send.at[n, 0])
-        for n, (source, target_ref) in enumerate(head_copies(0)[1])
-    ]
-    for copy in own:
-        copy.start()
-
-    def send_heads(step, carry):
-        for copy in head_remote(step):
-            copy.start()
-        return carry
-
-    lax.fori_loop(1, 8, send_heads, 0)
-
     def dispatch(g, carry):
         at = pl.ds(g * GROUP, GROUP)
         rows = pl.ds(pl.multiple_of(g * ROWS, ROWS), ROWS)
@@ -426,14 +427,16 @@
         send[at, :, WIDE : WIDE + TAIL] = x_tail.reshape(GROUP, 8, TAIL)
         send[at, :, WIDE + TAIL : MESSAGE] = h_tail.reshape(GROUP, 8, HEAD_SIZE)
 
-        def start(order, inner):
-            pltpu.make_async_remote_copy(
+        def start(step, inner):
+            order = first + lax.rem(step + turn, GROUP)
+            copy = pltpu.make_async_remote_copy(
                 src_ref=send.at[order], dst_ref=recv.at[order], send_sem=send_sem,
                 recv_sem=recv_sem.at[g], device_id=place_of(order, 1, here), device_id_type=MESH,
-            ).start()
+            )
+            pl.when(order > 0)(copy.start)
             return inner
 
-        lax.fori_loop(jnp.maximum(first, 1), first + GROUP, start, 0)
+        lax.fori_loop(0, GROUP, start, 0)
         return carry
 
     lax.fori_loop(0, GROUPS, dispatch, 0)
@@ -484,14 +487,16 @@
         tails = dot(spread, last_rows[...], NN).astype(bf16)
         back[at, :, D : D + TAIL] = tails.reshape(GROUP, 8, TAIL)
 
-        def start(order, inner):
-            pltpu.make_async_remote_copy(
+        def start(step, inner):
+            order = first + lax.rem(step + turn, GROUP)
+            copy = pltpu.make_async_remote_copy(
                 src_ref=back.at[order], dst_ref=back_recv.at[order], send_sem=back_sem,
                 recv_sem=back_recv_sem, device_id=place_of(order, -1, here), device_id_type=MESH,
-            ).start()
+            )
+            pl.when(order > 0)(copy.start)
             return inner
 
-        lax.fori_loop(jnp.maximum(first, 1), first + GROUP, start, 0)
+        lax.fori_loop(0, GROUP, start, 0)
         return carry
 
     lax.fori_loop(0, GROUPS, work, 0)
@@ -600,6 +605,30 @@
     )(state, gain, layer_grad, grads, routes, w_gate, w_up, queries, keys, values)
 
 
+def finish_kernel(count, *refs):
+    sources, targets, sems = refs[:count], refs[count : 2 * count], refs[2 * count]
+    copies = [
+        pltpu.make_async_copy(sources[n], targets[n], sems.at[n]) for n in range(count)
+    ]
+    for copy in copies:
+        copy.start()
+    for copy in copies:
+        copy.wait()
+
+
+def finish(*arrays):
+    hbm = pl.BlockSpec(memory_space=pl.ANY)
+    return pl.pallas_call(
+        functools.partial(finish_kernel, len(arrays)),
+        out_shape=tuple(jax.ShapeDtypeStruct(a.shape, a.dtype) for a in arrays),
+        in_specs=[hbm] * len(arrays),
+        out_specs=(hbm,) * len(arrays),
+        scratch_shapes=[pltpu.SemaphoreType.DMA((len(arrays),))],
+        compiler_params=pltpu.CompilerParams(vmem_limit_bytes=1 << 20),
+        name="finish",
+    )(*arrays)
+
+
 def local(
     queries,
     keys,
@@ -628,7 +657,8 @@
     query_out, key_out, value_out = attention_core(
         residual_rows, w_out, query_all, key_all, value_all
     )
-    return (query_out[None], key_out[None], value_out[None], residual_rows[None], gate_grad[None], up_grad[None])
+    outs = (query_out, key_out, value_out, residual_rows, gate_grad, up_grad)
+    return tuple(out[None] for out in finish(*outs))
 
 
 def solution(mesh):

time: 232 us -> 221 us (0.953); the launches traced: 229 us -> 220 us
  local copies, waits for them, and re-layouts: 11.1 us -> 3.04 us
    unnamed x12, local copies, waits for them, and re-layouts: 11.1 us -> 3.04 us
    pallas_call x1, Pallas kernels: 166 us -> 160 us  [expert_block(): pl.pallas_call(expert_kernel, out_shape=(jax.ShapeDtypeStruct((tokens, D)...]
    pallas_call x0 -> x1, Pallas kernels: none -> 3.35 us  [finish(): pl.pallas_call(functools.partial(finish_kernel, len(arrays)), out_shape=t...]
where the time goes in v4:
time: 221 us; the launch traced here: 220 us
  Pallas kernels  216 us (98%)
  local copies, waits for them, and re-layouts  3.04 us (1%)
    pallas_call x1, Pallas kernels, expert_block(): pl.pallas_call(expert_kernel, out_shape=(jax.ShapeDtypeStruct((tokens, D)...  160 us
    pallas_call x1, Pallas kernels, attention_core(): pl.pallas_call(attention_kernel, out_shape=(jax.ShapeDtypeStruct((tokens,...  52.3 us

profile of v4, /device:TPU:1, one launch (start us, length us, event | category | flops | bytes accessed | tf_op | source)
XLA Modules:
  0.0 219.9 jit_solution(9857839600711474712)
XLA Ops:
  0.6 160.3 %expert_block.1 = (bf16[128,2048]{1,0:T(8,128)(2,1)}, bf16[2048,768]{1,0:T(8,128)(2,1)}, bf16[2048,768]{1,0:T(8,128)(2,1)}, bf16[1024,512]{1,0:T(8,128)(2,1)}, b...) custom-call(bf16[128,2048]{1,0:T(8,128)(2,1)} %bitcast.25, bf16[16,128]{1,0:T(8,128)(2,1)} %bitcast.32, ...), custom_call_target="tpu_custom_call" | custom-call | flops 30000001024 | bytes 20000000 | tf_op jit(solution)/shard_map/expert_block/pallas_call | solution.py:562
  160.9 0.0 copy-start
  161.0 0.0 copy-start.1
  161.0 0.0 copy-start.3
  161.0 52.3 %attention_core.1 = (bf16[128,4096]{1,0:T(8,128)(2,1)}, bf16[128,512]{1,0:T(8,128)(2,1)}, bf16[128,512]{1,0:T(8,128)(2,1)}) custom-call(bf16[128,2048]{1,0:T(8,128)(2,1)} %get-tuple-element.21.residual_ref.refs_3_, bf16[512,2048]{1,0:T(8,128)(2,1)} %w_hbm.1, bf16[1024,512]{1,0:T(8,128)(2,1)} %get-tuple-element.22.query_hbm, ...), custom_call_target="tpu_custom_call" | custom-call | flops 8999999488 | bytes 10000000 | tf_op jit(solution)/shard_map/attention_core/pallas_call | solution.py:230
  213.3 0.0 copy-done
  213.3 0.0 copy-done.1
  213.3 0.0 copy-done.3
  213.3 0.0 copy-start.2
  213.3 1.2 copy-done.2
  214.6 0.0 copy-start.4
  214.6 0.9 copy-done.4
  215.5 0.0 copy-start.5
  215.5 0.9 copy-done.5
  216.4 3.4 %finish.1 = (bf16[128,4096]{1,0:T(8,128)(2,1)}, bf16[128,512]{1,0:T(8,128)(2,1)}, bf16[128,512]{1,0:T(8,128)(2,1)}, bf16[128,2048]{1,0:T(8,128)(2,1)}, bf16[2048...) custom-call(bf16[128,4096]{1,0:T(8,128)(2,1)S(1)} %copy-done.2, bf16[128,512]{1,0:T(8,128)(2,1)S(1)} %copy-done.4, ...), custom_call_target="tpu_custom_call" | custom-call | tf_op jit(solution)/shard_map/finish/pallas_call | solution.py:621
Async XLA Ops:
  160.9 52.4 %copy-start = (bf16[2048,768]{1,0:T(8,128)(2,1)S(1)}, bf16[2048,768]{1,0:T(8,128)(2,1)}, u32[]{:S(2)}) copy-start(bf16[2048,768]{1,0:T(8,128)(2,1)} %get-tuple-element.28.refs_4_) | copy-start | bytes 9437188
  161.0 52.4 %copy-start.1 = (bf16[2048,768]{1,0:T(8,128)(2,1)S(1)}, bf16[2048,768]{1,0:T(8,128)(2,1)}, u32[]{:S(2)}) copy-start(bf16[2048,768]{1,0:T(8,128)(2,1)} %get-tuple-element.29.refs_5_) | copy-start | bytes 9437188
  161.0 52.4 %copy-start.3 = (bf16[128,2048]{1,0:T(8,128)(2,1)S(1)}, bf16[128,2048]{1,0:T(8,128)(2,1)}, u32[]{:S(2)}) copy-start(bf16[128,2048]{1,0:T(8,128)(2,1)} %get-tuple-element.21.residual_ref.refs_3_) | copy-start | bytes 1572868
  213.3 1.2 copy-start.2
  214.6 0.9 copy-start.4
  215.5 0.9 copy-start.5

commit v5 on v4

--- a/solution.py
+++ b/solution.py
@@ -301,7 +301,7 @@
     state_ref, gain_ref, layer_ref, grads_ref, routes_ref, gate_hbm, up_hbm, query_hbm, key_hbm,
     value_hbm, residual_ref, gate_out, up_out, query_all, key_all, value_all,
     send, recv, back, back_recv, weights, rows_in, parts, stage, expert_in, hot, hot_t, last,
-    codes, last_rows, weight_sem, send_sem, recv_sem, back_sem, back_recv_sem, out_sem,
+    codes, last_rows, total, weight_sem, send_sem, recv_sem, back_sem, back_recv_sem, out_sem,
     head_send, head_recv,
 ):
     seq, expert = lax.axis_index("seq"), lax.axis_index("expert")
@@ -362,12 +362,25 @@
     for copy in own:
         copy.start()
 
-    def send_heads(step, carry):
-        for copy in head_remote(step):
+    for step in (2, 6, 4, 1, 3, 5, 7):
+        copies = head_remote(step)
+        for copy in copies if step in (1, 2, 4, 6) else copies[:1]:
             copy.start()
-        return carry
-
-    lax.fori_loop(1, 8, send_heads, 0)
+
+    def hand_on(dx):
+        rows = pl.ds(
+            pl.multiple_of((lax.rem(here[0] + 4 - dx, 4) * 2 + here[1]) * tokens, tokens), tokens
+        )
+        mate = here[0] * 2 + 1 - here[1]
+        return [
+            pltpu.make_async_remote_copy(
+                src_ref=array.at[rows, :], dst_ref=array.at[rows, :],
+                send_sem=head_send.at[n, 2 * dx + 1], recv_sem=head_recv.at[n, 2 * dx + 1],
+                device_id=(mate, expert), device_id_type=MESH,
+            )
+            for n, array in ((1, key_all), (2, value_all))
+        ]
+
 
     lanes = iota((tokens, 128), 1)
     route = routes_ref[...].astype(f32).T
@@ -491,7 +504,7 @@
             order = first + lax.rem(step + turn, GROUP)
             copy = pltpu.make_async_remote_copy(
                 src_ref=back.at[order], dst_ref=back_recv.at[order], send_sem=back_sem,
-                recv_sem=back_recv_sem, device_id=place_of(order, -1, here), device_id_type=MESH,
+                recv_sem=back_recv_sem.at[g], device_id=place_of(order, -1, here), device_id_type=MESH,
             )
             pl.when(order > 0)(copy.start)
             return inner
@@ -500,7 +513,13 @@
         return carry
 
     lax.fori_loop(0, GROUPS, work, 0)
-    pltpu.make_async_copy(back.at[0], back_recv.at[0], back_recv_sem).start()
+    pltpu.make_async_copy(back.at[0], back_recv.at[0], back_recv_sem.at[0]).start()
+
+    for dx in (1, 3, 2):
+        for copy in head_remote(2 * dx)[1:]:
+            copy.wait_recv()
+        for copy in hand_on(dx):
+            copy.start()
 
     def weight_grads(f, carry):
         tile = pl.ds(pl.multiple_of(f * 256, 256), 256)
@@ -515,18 +534,30 @@
 
     lax.fori_loop(0, 8, weight_grads, 0)
 
-    pltpu.make_async_copy(back_recv, back_recv, back_recv_sem).wait()
-    slot_of = lax.rem(iota((tokens, 1024), 1), 8)
+    slot_of = lax.rem(iota((tokens, ROWS), 1), 8)
+    total[...] = jnp.zeros_like(total)
+
+    def combine(g, carry):
+        at = pl.ds(g * GROUP, GROUP)
+        pltpu.make_async_copy(back_recv.at[at], back_recv.at[at], back_recv_sem.at[g]).wait()
+        hot_part = hot_t[:, pl.ds(pl.multiple_of(g * ROWS, ROWS), ROWS)]
+        last_part = hot_t[:, pl.ds(pl.multiple_of(1024 + g * ROWS, ROWS), ROWS)]
+        tails = back_recv[at, :, D : D + TAIL].reshape(ROWS, TAIL)
+        for n in range(8):
+            tile = slice(n * 256, (n + 1) * 256)
+            routed = dot(hot_part, back_recv[at, :, tile].reshape(ROWS, 256), NN)
+            chosen = jnp.where(slot_of == n, last_part, jnp.zeros((), bf16))
+            total[:, tile] += routed + dot(chosen, tails, NN)
+        return carry
+
+    lax.fori_loop(0, GROUPS, combine, 0)
     state = state_ref[...].astype(f32)
     rstd = lax.rsqrt(jnp.mean(state * state, axis=-1, keepdims=True) + 1e-06)
     inner = jnp.zeros((tokens, 1), f32)
     weighted = []
     for n in range(8):
         tile = slice(n * 256, (n + 1) * 256)
-        routed = dot(hot_t[:, 0:1024], back_recv[:, :, tile].reshape(1024, 256), NN)
-        chosen = jnp.where(slot_of == n, hot_t[:, 1024:2048], jnp.zeros((), bf16))
-        routed += dot(chosen, back_recv[:, :, D : D + TAIL].reshape(1024, TAIL), NN)
-        weighted.append(gain[:, tile] * routed)
+        weighted.append(gain[:, tile] * total[:, tile])
         inner += jnp.sum(weighted[n] * (state[:, tile] * rstd), axis=-1, keepdims=True)
     inner = inner * (1.0 / D)
     for n in range(8):
@@ -545,12 +576,18 @@
     for copy in own:
         copy.wait()
 
-    def finish_heads(step, carry):
-        for copy in head_remote(step):
-            copy.wait()
-        return carry
-
-    lax.fori_loop(1, 8, finish_heads, 0)
+    for step in range(1, 8):
+        copies = head_remote(step)
+        copies[0].wait()
+        if step == 1:
+            for copy in copies[1:]:
+                copy.wait()
+        elif step % 2 == 0:
+            for copy in copies[1:]:
+                copy.wait_send()
+        else:
+            for copy in hand_on(step // 2):
+                copy.wait()
 
 
 def expert_block(state, gain, layer_grad, grads, routes, w_gate, w_up, queries, keys, values):
@@ -586,11 +623,12 @@
             pltpu.VMEM((128, tokens), bf16),
             pltpu.VMEM((1, tokens * TOP), f32),
             pltpu.VMEM((ROWS, TAIL), bf16),
+            pltpu.VMEM((tokens, D), f32),
             dma((2,)),
             dma,
             dma((GROUPS,)),
             dma,
-            dma,
+            dma((GROUPS,)),
             dma((2,)),
             dma((3, 8)),
             dma((3, 8)),

time: 221 us -> 218 us (0.986)
  Pallas kernels: 216 us -> 212 us
    pallas_call x1, Pallas kernels: 160 us -> 157 us  [expert_block(): pl.pallas_call(expert_kernel, out_shape=(jax.ShapeDtypeStruct((tokens, D)...]
where the time goes in v5:
time: 218 us; the launch traced here: 216 us
  Pallas kernels  212 us (97%)
  local copies, waits for them, and re-layouts  3.04 us (1%)
    pallas_call x1, Pallas kernels, expert_block(): pl.pallas_call(expert_kernel, out_shape=(jax.ShapeDtypeStruct((tokens, D)...  157 us
    pallas_call x1, Pallas kernels, attention_core(): pl.pallas_call(attention_kernel, out_shape=(jax.ShapeDtypeStruct((tokens,...  52.3 us

profile of v5, /device:TPU:1, one launch (start us, length us, event | category | flops | bytes accessed | tf_op | source)
XLA Modules:
  0.0 216.2 jit_solution(10421973282551670648)
XLA Ops:
  0.6 156.6 %expert_block.1 = (bf16[128,2048]{1,0:T(8,128)(2,1)}, bf16[2048,768]{1,0:T(8,128)(2,1)}, bf16[2048,768]{1,0:T(8,128)(2,1)}, bf16[1024,512]{1,0:T(8,128)(2,1)}, b...) custom-call(bf16[128,2048]{1,0:T(8,128)(2,1)} %bitcast.25, bf16[16,128]{1,0:T(8,128)(2,1)} %bitcast.32, ...), custom_call_target="tpu_custom_call" | custom-call | flops 30000001024 | bytes 20000000 | tf_op jit(solution)/shard_map/expert_block/pallas_call | solution.py:599
  157.3 0.0 copy-start
  157.3 0.0 copy-start.1
  157.3 0.0 copy-start.3
  157.3 52.3 %attention_core.1 = (bf16[128,4096]{1,0:T(8,128)(2,1)}, bf16[128,512]{1,0:T(8,128)(2,1)}, bf16[128,512]{1,0:T(8,128)(2,1)}) custom-call(bf16[128,2048]{1,0:T(8,128)(2,1)} %get-tuple-element.21.residual_ref.refs_3_, bf16[512,2048]{1,0:T(8,128)(2,1)} %w_hbm.1, bf16[1024,512]{1,0:T(8,128)(2,1)} %get-tuple-element.22.query_hbm, ...), custom_call_target="tpu_custom_call" | custom-call | flops 8999999488 | bytes 10000000 | tf_op jit(solution)/shard_map/attention_core/pallas_call | solution.py:230
  209.6 0.0 copy-done
  209.6 0.0 copy-done.1
  209.6 0.0 copy-done.3
  209.6 0.0 copy-start.2
  209.6 1.2 copy-done.2
  210.9 0.0 copy-start.4
  210.9 0.9 copy-done.4
  211.8 0.0 copy-start.5
  211.8 0.9 copy-done.5
  212.7 3.4 %finish.1 = (bf16[128,4096]{1,0:T(8,128)(2,1)}, bf16[128,512]{1,0:T(8,128)(2,1)}, bf16[128,512]{1,0:T(8,128)(2,1)}, bf16[128,2048]{1,0:T(8,128)(2,1)}, bf16[2048...) custom-call(bf16[128,4096]{1,0:T(8,128)(2,1)S(1)} %copy-done.2, bf16[128,512]{1,0:T(8,128)(2,1)S(1)} %copy-done.4, ...), custom_call_target="tpu_custom_call" | custom-call | tf_op jit(solution)/shard_map/finish/pallas_call | solution.py:659
Async XLA Ops:
  157.3 52.3 %copy-start = (bf16[2048,768]{1,0:T(8,128)(2,1)S(1)}, bf16[2048,768]{1,0:T(8,128)(2,1)}, u32[]{:S(2)}) copy-start(bf16[2048,768]{1,0:T(8,128)(2,1)} %get-tuple-element.28.refs_4_) | copy-start | bytes 9437188
  157.3 52.3 %copy-start.1 = (bf16[2048,768]{1,0:T(8,128)(2,1)S(1)}, bf16[2048,768]{1,0:T(8,128)(2,1)}, u32[]{:S(2)}) copy-start(bf16[2048,768]{1,0:T(8,128)(2,1)} %get-tuple-element.29.refs_5_) | copy-start | bytes 9437188
  157.3 52.3 %copy-start.3 = (bf16[128,2048]{1,0:T(8,128)(2,1)S(1)}, bf16[128,2048]{1,0:T(8,128)(2,1)}, u32[]{:S(2)}) copy-start(bf16[128,2048]{1,0:T(8,128)(2,1)} %get-tuple-element.21.residual_ref.refs_3_) | copy-start | bytes 1572868
  209.6 1.2 copy-start.2
  210.9 0.9 copy-start.4
  211.8 0.9 copy-start.5

commit v6 on v5

--- a/solution.py
+++ b/solution.py
@@ -144,9 +144,9 @@
         copy.wait_recv()
     project(device(2, 1))
 
-    def backward_block(i):
+    def backward_block(i, part):
         lower, upper = i * block, (i + 1) * block
-        for head in range(4):
+        for head in (2 * part, 2 * part + 1):
             columns = slice(head * HEAD_SIZE, (head + 1) * HEAD_SIZE)
             out_grad = grad[lower:upper, columns]
             prob = probs[i][head]
@@ -160,11 +160,14 @@
 
     pair = slice(4 * HEAD_SIZE, 6 * HEAD_SIZE)
 
-    def query_copy(dx, dc):
-        to, number = device(dx, dc), dx * 2 + dc
+    def own_columns(part):
+        return pl.ds(pl.multiple_of(seq * 512 + part * 256, 256), 256)
+
+    def query_copy(dx, dc, part):
+        to, number = device(dx, dc), part * 8 + dx * 2 + dc
         return pltpu.make_async_remote_copy(
-            src_ref=packed.at[rows_of(to, 0, tokens), pl.ds(0, 512)],
-            dst_ref=query_out.at[:, pl.ds(pl.multiple_of(seq * 512, 512), 512)],
+            src_ref=packed.at[rows_of(to, 0, tokens), pl.ds(part * 256, 256)],
+            dst_ref=query_out.at[:, own_columns(part)],
             send_sem=query_send.at[number], recv_sem=query_recv.at[number],
             device_id=(to, expert), device_id_type=MESH,
         )
@@ -178,27 +181,24 @@
             device_id=(to, expert), device_id_type=MESH,
         )
 
-    own_query = pltpu.make_async_copy(
-        packed.at[rows_of(seq, 0, tokens), pl.ds(0, 512)],
-        query_out.at[:, pl.ds(pl.multiple_of(seq * 512, 512), 512)],
-        query_send.at[0],
-    )
+    own_query = [
+        pltpu.make_async_copy(
+            packed.at[rows_of(seq, 0, tokens), pl.ds(part * 256, 256)],
+            query_out.at[:, own_columns(part)],
+            query_send.at[part * 8],
+        )
+        for part in range(2)
+    ]
 
     def backward_step(step, carry):
         dx = lax.rem(step + 1, 4)
         chip = lax.rem(x + dx, 4)
-        for i in range(4):
-            pl.when(chip == i)(functools.partial(backward_block, i))
-
-        @pl.when(step < 3)
-        def _():
-            query_copy(dx, 0).start()
-
-        @pl.when(step == 3)
-        def _():
-            own_query.start()
-
-        query_copy(dx, 1).start()
+        for part in range(2):
+            for i in range(4):
+                pl.when(chip == i)(functools.partial(backward_block, i, part))
+            pl.when(step < 3)(query_copy(dx, 0, part).start)
+            pl.when(step == 3)(own_query[part].start)
+            query_copy(dx, 1, part).start()
         return carry
 
     lax.fori_loop(0, 4, backward_step, 0)
@@ -217,9 +217,11 @@
     for copy in copies:
         copy.wait_send()
     for step in range(1, 8):
-        query_copy(step // 2, step % 2).wait()
+        for part in range(2):
+            query_copy(step // 2, step % 2, part).wait()
         pair_copy(step // 2, step % 2).wait_send()
-    own_query.wait()
+    for copy in own_query:
+        copy.wait()
 
 
 def attention_core(residual, w_out, queries, keys, values):
@@ -255,8 +257,8 @@
             dma((4,)),
             dma((13,)),
             dma((13,)),
-            dma((8,)),
-            dma((8,)),
+            dma((16,)),
+            dma((16,)),
             dma((8,)),
             dma((8,)),
         ],
@@ -306,7 +308,7 @@
 ):
     seq, expert = lax.axis_index("seq"), lax.axis_index("expert")
     here = (seq // 2, lax.rem(seq, 2), expert // 4, lax.rem(expert, 4))
-    turn = seq * 13 + expert * 7
+    turn = seq * 4 + expert * 2 + expert // 4
     tokens = state_ref.shape[0]
     bf16, f32 = jnp.bfloat16, jnp.float32
 

time: 218 us -> 217 us (level)
  no operation moved by 1% of the time
where the time goes in v6:
time: 217 us
  Pallas kernels  213 us (98%)
  local copies, waits for them, and re-layouts  3.04 us (1%)
    pallas_call x1, Pallas kernels, expert_block(): pl.pallas_call(expert_kernel, out_shape=(jax.ShapeDtypeStruct((tokens, D)...  157 us
    pallas_call x1, Pallas kernels, attention_core(): pl.pallas_call(attention_kernel, out_shape=(jax.ShapeDtypeStruct((tokens,...  52.7 us

profile of v6, /device:TPU:1, one launch (start us, length us, event | category | flops | bytes accessed | tf_op | source)
XLA Modules:
  0.0 216.6 jit_solution(4791381507213898828)
XLA Ops:
  0.6 156.6 %expert_block.1 = (bf16[128,2048]{1,0:T(8,128)(2,1)}, bf16[2048,768]{1,0:T(8,128)(2,1)}, bf16[2048,768]{1,0:T(8,128)(2,1)}, bf16[1024,512]{1,0:T(8,128)(2,1)}, b...) custom-call(bf16[128,2048]{1,0:T(8,128)(2,1)} %bitcast.25, bf16[16,128]{1,0:T(8,128)(2,1)} %bitcast.32, ...), custom_call_target="tpu_custom_call" | custom-call | flops 30000001024 | bytes 20000000 | tf_op jit(solution)/shard_map/expert_block/pallas_call | solution.py:601
  157.3 0.0 copy-start
  157.3 0.0 copy-start.1
  157.3 0.0 copy-start.3
  157.3 52.7 %attention_core.1 = (bf16[128,4096]{1,0:T(8,128)(2,1)}, bf16[128,512]{1,0:T(8,128)(2,1)}, bf16[128,512]{1,0:T(8,128)(2,1)}) custom-call(bf16[128,2048]{1,0:T(8,128)(2,1)} %get-tuple-element.21.residual_ref.refs_3_, bf16[512,2048]{1,0:T(8,128)(2,1)} %w_hbm.1, bf16[1024,512]{1,0:T(8,128)(2,1)} %get-tuple-element.22.query_hbm, ...), custom_call_target="tpu_custom_call" | custom-call | flops 8999999488 | bytes 10000000 | tf_op jit(solution)/shard_map/attention_core/pallas_call | solution.py:232
  210.0 0.0 copy-done
  210.0 0.0 copy-done.1
  210.0 0.0 copy-done.3
  210.0 0.0 copy-start.2
  210.1 1.2 copy-done.2
  211.3 0.0 copy-start.4
  211.3 0.9 copy-done.4
  212.2 0.0 copy-start.5
  212.2 0.9 copy-done.5
  213.1 3.4 %finish.1 = (bf16[128,4096]{1,0:T(8,128)(2,1)}, bf16[128,512]{1,0:T(8,128)(2,1)}, bf16[128,512]{1,0:T(8,128)(2,1)}, bf16[128,2048]{1,0:T(8,128)(2,1)}, bf16[2048...) custom-call(bf16[128,4096]{1,0:T(8,128)(2,1)S(1)} %copy-done.2, bf16[128,512]{1,0:T(8,128)(2,1)S(1)} %copy-done.4, ...), custom_call_target="tpu_custom_call" | custom-call | tf_op jit(solution)/shard_map/finish/pallas_call | solution.py:661
Async XLA Ops:
  157.3 52.7 %copy-start = (bf16[2048,768]{1,0:T(8,128)(2,1)S(1)}, bf16[2048,768]{1,0:T(8,128)(2,1)}, u32[]{:S(2)}) copy-start(bf16[2048,768]{1,0:T(8,128)(2,1)} %get-tuple-element.28.refs_4_) | copy-start | bytes 9437188
  157.3 52.7 %copy-start.1 = (bf16[2048,768]{1,0:T(8,128)(2,1)S(1)}, bf16[2048,768]{1,0:T(8,128)(2,1)}, u32[]{:S(2)}) copy-start(bf16[2048,768]{1,0:T(8,128)(2,1)} %get-tuple-element.29.refs_5_) | copy-start | bytes 9437188
  157.3 52.7 %copy-start.3 = (bf16[128,2048]{1,0:T(8,128)(2,1)S(1)}, bf16[128,2048]{1,0:T(8,128)(2,1)}, u32[]{:S(2)}) copy-start(bf16[128,2048]{1,0:T(8,128)(2,1)} %get-tuple-element.21.residual_ref.refs_3_) | copy-start | bytes 1572868
  210.0 1.2 copy-start.2
  211.3 0.9 copy-start.4
  212.2 0.9 copy-start.5
